TPU v7x, 128 devices: a whole 4x4x4 slice. The times are simulated.
128 devices in a mesh: ctx: 8 (over z, core), fsdp: 16 (over y, x).
Axes of the slice: x: 4, y: 4, z: 4, core: 2. Of those that a mesh axis runs over, the one named last changes fastest.
Arguments:
- tokens: bfloat16 [16, 2, 1024, 1024], P('fsdp', None, 'ctx'), may hold values from -6 to 6
- routes: int32 [16, 2, 1024, 8], P('fsdp', None, 'ctx'), may hold values from 0 to 31, all different within a row; in each aligned block of 128 rows (0 to 127, 128 to 255, ..., all dimensions but the last counted through in order) at most 40 rows name the same one
- doc_starts: int32 [16, 2, 1024], P('fsdp', None, 'ctx'), may hold values from 0 to 2047, as said below
- attn_gain: bfloat16 [1024], P('fsdp'), may hold values from 0.099609375 to 1.8984375
- attn_q: bfloat16 [1024, 1024], P('fsdp'), may hold values from -0.1875 to 0.1875
- attn_k: bfloat16 [1024, 512], P('fsdp'), may hold values from -0.1875 to 0.1875
- attn_v: bfloat16 [1024, 512], P('fsdp'), may hold values from -0.1875 to 0.1875
- attn_out: bfloat16 [1024, 1024], P('fsdp'), may hold values from -0.75 to 0.75
- ffn_gain: bfloat16 [1024], P('fsdp'), may hold values from 0.099609375 to 1.8984375
- router: bfloat16 [1024, 32], P('fsdp'), may hold values from -0.09375 to 0.09375
- w_gate: bfloat16 [32, 1024, 512], P('ctx', 'fsdp'), may hold values from -0.1875 to 0.1875
- w_up: bfloat16 [32, 1024, 512], P('ctx', 'fsdp'), may hold values from -0.1875 to 0.1875
- w_down: bfloat16 [32, 512, 1024], P('ctx', 'fsdp'), may hold values from -1 to 1
- cotangent: bfloat16 [16, 2, 1024, 1024], P('fsdp', None, 'ctx'), may hold values from -6 to 6
Outputs:
- mixed: bfloat16 [16, 2, 1024, 1024], P('fsdp', None, 'ctx')
- d_tokens: float32 [16, 2, 1024, 1024], P('fsdp', None, 'ctx')
- d_attn_gain: float32 [1024], P('fsdp')
- d_attn_q: float32 [1024, 1024], P('fsdp')
- d_attn_k: float32 [1024, 512], P('fsdp')
- d_attn_v: float32 [1024, 512], P('fsdp')
- d_attn_out: float32 [1024, 1024], P('fsdp')
- d_ffn_gain: float32 [1024], P('fsdp')
- d_router: float32 [1024, 32], P('fsdp')
- d_w_gate: float32 [32, 1024, 512], P('ctx', 'fsdp')
- d_w_up: float32 [32, 1024, 512], P('ctx', 'fsdp')
- d_w_down: float32 [32, 512, 1024], P('ctx', 'fsdp')
Inputs may be any that keep to these rules, and one draw needn't show every extreme that they name: `routes`: each row names 8 different experts; in the 128 rows of one device in one micro-batch no expert is named more than 40 times, a bound that some block reaches in some of them. doc_starts at position p is 0 for p = 0 and otherwise p or its value at p - 1; in every stream one document covers a whole micro-batch.
All inputs are finite; a program needn't handle non-finite values.
Results may differ from a plain program's by a relative error of at most 0.025.
Values may be sent and summed in bfloat16 or wider, within the bound.
No kernel may reach another device: no remote copies, remote signals or barrier semaphores. Data moves between devices by JAX's collectives and lax.ppermute only.
A program may use at most 256 MiB of HBM per device.

v0:
```python
import math

import jax
import jax.numpy as jnp
from jax import lax
from jax.sharding import PartitionSpec as P

HEADS = 16
KV_HEADS = 8
HEAD_DIM = 64
MICRO = 2


EPSILON = 1e-06
HIGHEST = lax.Precision.HIGHEST


def normalize(values):
    scale_rows = lax.rsqrt(jnp.mean(values * values, -1, keepdims=True) + EPSILON)
    return (values * scale_rows, scale_rows)


def norm_back(grad_norm, normed, scale_rows):
    return scale_rows * (grad_norm - normed * jnp.mean(grad_norm * normed, -1, keepdims=True))


def angles(positions):
    half_width = HEAD_DIM // 2
    frequencies = 10000.0 ** (-2.0 * jnp.arange(half_width, dtype=jnp.float32) / HEAD_DIM)
    turned = positions.astype(jnp.float32)[:, None] * frequencies[None, :]
    return (jnp.cos(turned)[:, None, :], jnp.sin(turned)[:, None, :])


def rotate(values, cosine_rows, sine_rows):
    half_width = values.shape[-1] // 2
    front_half = values[..., :half_width]
    back_half = values[..., half_width:]
    return jnp.concatenate(
        [
            front_half * cosine_rows - back_half * sine_rows,
            back_half * cosine_rows + front_half * sine_rows,
        ],
        -1,
    )


def rotate_back(grads_in, cosine_rows, sine_rows):
    half_width = grads_in.shape[-1] // 2
    front_half = grads_in[..., :half_width]
    back_half = grads_in[..., half_width:]
    return jnp.concatenate(
        [
            front_half * cosine_rows + back_half * sine_rows,
            back_half * cosine_rows - front_half * sine_rows,
        ],
        -1,
    )


def masked_scores(queries, gathered, positions, starts, span_count, batch_len):
    kv_width = KV_HEADS * HEAD_DIM
    key_part = gathered[..., :kv_width].reshape(-1, KV_HEADS, HEAD_DIM)
    grouped = queries.reshape(queries.shape[0], KV_HEADS, HEADS // KV_HEADS, HEAD_DIM)
    scores = jnp.einsum("qgcd,jgd->gcqj", grouped, key_part, preferred_element_type=jnp.float32) * (
        1.0 / math.sqrt(HEAD_DIM)
    )
    key_pos = (
        jnp.arange(span_count, dtype=jnp.int32)[None, :] * batch_len
        + jnp.arange(gathered.shape[0], dtype=jnp.int32)[:, None]
    ).reshape(-1)
    visible = (key_pos[None, :] >= starts[:, None]) & (key_pos[None, :] <= positions[:, None])
    return jnp.where(visible[None, None], scores, -jnp.inf)


def per_device(
    tokens,
    routes,
    doc_starts,
    attn_gain,
    attn_q,
    attn_k,
    attn_v,
    attn_out,
    ffn_gain,
    router,
    w_gate,
    w_up,
    w_down,
    cotangent,
):
    rows_dev = tokens.shape[2]
    model_width = tokens.shape[3]
    top_count = routes.shape[3]
    experts = router.shape[1]
    local_experts = w_gate.shape[0]
    ctx_count = lax.axis_size("ctx")
    ctx_rank = lax.axis_index("ctx")
    batch_len = rows_dev * ctx_count
    capacity = 5 * rows_dev * top_count // (4 * experts)
    slot_count = experts * capacity
    kv_width = KV_HEADS * HEAD_DIM
    group_size = HEADS // KV_HEADS
    inverse_root = 1.0 / math.sqrt(HEAD_DIM)
    params = (attn_gain, attn_q, attn_k, attn_v, attn_out, ffn_gain, router, w_gate, w_up, w_down)

    def current():
        return (
            lax.all_gather(params[0], "fsdp", axis=0, tiled=True),
            lax.all_gather(params[1], "fsdp", axis=0, tiled=True),
            lax.all_gather(params[2], "fsdp", axis=0, tiled=True),
            lax.all_gather(params[3], "fsdp", axis=0, tiled=True),
            lax.all_gather(params[4], "fsdp", axis=0, tiled=True),
            lax.all_gather(params[5], "fsdp", axis=0, tiled=True),
            lax.all_gather(params[6], "fsdp", axis=0, tiled=True),
            lax.all_gather(params[7], "fsdp", axis=1, tiled=True),
            lax.all_gather(params[8], "fsdp", axis=1, tiled=True),
            lax.all_gather(params[9], "fsdp", axis=1, tiled=True),
        )

    def all_keys(own_rows):
        return lax.all_gather(own_rows, "ctx", axis=0, tiled=True)

    def to_owners(slot_rows):
        return lax.all_to_all(slot_rows, "ctx", split_axis=0, concat_axis=0, tiled=True)

    def to_sources(slot_rows):
        return lax.all_to_all(slot_rows, "ctx", split_axis=0, concat_axis=0, tiled=True)

    slot_ids = jnp.arange(slot_count, dtype=jnp.int32)
    expert_ids = jnp.arange(experts, dtype=jnp.int32)
    key_store = []
    kept_state = []
    mixed_parts = []
    for batch_index in range(MICRO):
        (
            gain_one,
            weight_q,
            weight_k,
            weight_v,
            weight_o,
            gain_two,
            weight_r,
            weight_g,
            weight_u,
            weight_d,
        ) = current()
        inputs = tokens[0, batch_index].astype(jnp.float32)
        normed, scale_rows = normalize(inputs)
        hidden_in = (normed * gain_one.astype(jnp.float32)).astype(jnp.bfloat16)
        query_lin = jnp.dot(hidden_in, weight_q, preferred_element_type=jnp.float32)
        key_lin = jnp.dot(hidden_in, weight_k, preferred_element_type=jnp.float32)
        values = jnp.dot(hidden_in, weight_v, preferred_element_type=jnp.float32).astype(
            jnp.bfloat16
        )
        positions = (
            batch_index * batch_len + ctx_rank * rows_dev + jnp.arange(rows_dev, dtype=jnp.int32)
        )
        cosine_rows, sine_rows = angles(positions)
        queries = rotate(
            query_lin.reshape(rows_dev, HEADS, HEAD_DIM), cosine_rows, sine_rows
        ).astype(jnp.bfloat16)
        keys_now = (
            rotate(key_lin.reshape(rows_dev, KV_HEADS, HEAD_DIM), cosine_rows, sine_rows)
            .astype(jnp.bfloat16)
            .reshape(rows_dev, kv_width)
        )
        key_store.append(jnp.concatenate([keys_now, values], -1))
        gathered = all_keys(jnp.stack(key_store, 1))
        starts = doc_starts[0, batch_index]
        scores = masked_scores(queries, gathered, positions, starts, batch_index + 1, batch_len)
        log_total = jax.nn.logsumexp(scores, -1)
        weights_low = jnp.exp(scores - log_total[..., None]).astype(jnp.bfloat16)
        value_part = gathered[..., kv_width:].reshape(-1, KV_HEADS, HEAD_DIM)
        attended = jnp.einsum(
            "gcqj,jgd->qgcd", weights_low, value_part, preferred_element_type=jnp.float32
        )
        attended = attended.reshape(rows_dev, HEADS * HEAD_DIM).astype(jnp.bfloat16)
        residual = inputs + jnp.dot(attended, weight_o, preferred_element_type=jnp.float32)
        normed_two, scale_two = normalize(residual)
        hidden_two = (normed_two * gain_two.astype(jnp.float32)).astype(jnp.bfloat16)
        logits = jnp.dot(
            hidden_two.astype(jnp.float32), weight_r.astype(jnp.float32), precision=HIGHEST
        )
        route_rows = routes[0, batch_index]
        gate_rows = jax.nn.softmax(jnp.take_along_axis(logits, route_rows, 1), -1)
        chosen = route_rows[:, :, None] == expert_ids[None, None, :]
        flat_hits = chosen.reshape(rows_dev * top_count, experts).astype(jnp.int32)
        rank_rows = jnp.sum(jnp.cumsum(flat_hits, 0) * flat_hits, -1) - 1
        slot_index = (route_rows.reshape(-1) * capacity + rank_rows).reshape(rows_dev, top_count)
        matches = slot_index[None, :, :] == slot_ids[:, None, None]
        dispatch = jnp.any(matches, -1).astype(jnp.bfloat16)
        sent = jnp.dot(dispatch, hidden_two, preferred_element_type=jnp.float32).astype(
            jnp.bfloat16
        )
        received = to_owners(sent.reshape(ctx_count, local_experts, capacity, model_width))
        gate_lin = jnp.einsum(
            "secd,edf->secf", received, weight_g, preferred_element_type=jnp.float32
        )
        up_lin = jnp.einsum(
            "secd,edf->secf", received, weight_u, preferred_element_type=jnp.float32
        )
        inner_act = (gate_lin * jax.nn.sigmoid(gate_lin) * up_lin).astype(jnp.bfloat16)
        expert_out = jnp.einsum(
            "secf,efd->secd", inner_act, weight_d, preferred_element_type=jnp.float32
        ).astype(jnp.bfloat16)
        returned = to_sources(expert_out).reshape(slot_count, model_width)
        picked_out = returned[slot_index]
        mixture = jnp.einsum("tk,tkd->td", gate_rows, picked_out.astype(jnp.float32))
        mixed_parts.append((residual + mixture).astype(jnp.bfloat16))
        kept_state.append(
            (
                hidden_in,
                queries,
                log_total,
                attended,
                residual,
                hidden_two,
                gate_rows,
                chosen,
                matches,
                dispatch,
                received,
                gate_lin,
                up_lin,
                inner_act,
                picked_out,
            )
        )
    grad_sums = [None] * 10
    key_grads = [
        jnp.zeros((rows_dev, MICRO * 0 + 2 * kv_width), jnp.float32) for batch_index in range(MICRO)
    ]
    input_grads = [None] * MICRO
    for batch_index in reversed(range(MICRO)):
        (
            gain_one,
            weight_q,
            weight_k,
            weight_v,
            weight_o,
            gain_two,
            weight_r,
            weight_g,
            weight_u,
            weight_d,
        ) = current()
        (
            hidden_in,
            queries,
            log_total,
            attended,
            residual,
            hidden_two,
            gate_rows,
            chosen,
            matches,
            dispatch,
            received,
            gate_lin,
            up_lin,
            inner_act,
            picked_out,
        ) = kept_state[batch_index]
        grad_low = cotangent[0, batch_index]
        grad_out = grad_low.astype(jnp.float32)
        slot_gate = jnp.sum(jnp.where(matches, gate_rows[None, :, :], 0.0), (1, 2))
        grad_slots = jnp.dot(dispatch, grad_low, preferred_element_type=jnp.float32)
        grad_y = (grad_slots * slot_gate[:, None]).astype(jnp.bfloat16)
        grad_recv = to_owners(grad_y.reshape(ctx_count, local_experts, capacity, model_width))
        grad_inner = jnp.einsum(
            "secd,efd->secf", grad_recv, weight_d, preferred_element_type=jnp.float32
        )
        sigmoid_gate = jax.nn.sigmoid(gate_lin)
        grad_gate = (
            grad_inner * up_lin * sigmoid_gate * (1.0 + gate_lin * (1.0 - sigmoid_gate))
        ).astype(jnp.bfloat16)
        grad_up = (grad_inner * gate_lin * sigmoid_gate).astype(jnp.bfloat16)
        grad_taken = jnp.einsum(
            "secf,edf->secd", grad_gate, weight_g, preferred_element_type=jnp.float32
        )
        grad_taken = (
            grad_taken
            + jnp.einsum("secf,edf->secd", grad_up, weight_u, preferred_element_type=jnp.float32)
        ).astype(jnp.bfloat16)
        d_gate_w = jnp.einsum(
            "secd,secf->edf", received, grad_gate, preferred_element_type=jnp.float32
        )
        d_up_w = jnp.einsum("secd,secf->edf", received, grad_up, preferred_element_type=jnp.float32)
        d_down_w = jnp.einsum(
            "secf,secd->efd", inner_act, grad_recv, preferred_element_type=jnp.float32
        )
        grad_back = to_sources(grad_taken).reshape(slot_count, model_width)
        grad_pick = jnp.einsum("td,tkd->tk", grad_out, picked_out.astype(jnp.float32))
        grad_select = gate_rows * (grad_pick - jnp.sum(gate_rows * grad_pick, -1, keepdims=True))
        grad_logits = jnp.einsum("tk,tke->te", grad_select, chosen.astype(jnp.float32))
        d_router_w = jnp.dot(hidden_two.astype(jnp.float32).T, grad_logits, precision=HIGHEST)
        grad_two = jnp.einsum("st,sd->td", dispatch, grad_back, preferred_element_type=jnp.float32)
        grad_two = grad_two + jnp.dot(
            grad_logits, weight_r.astype(jnp.float32).T, precision=HIGHEST
        )
        normed_two, scale_two = normalize(residual)
        d_gain_two = jnp.sum(grad_two * normed_two, 0)
        grad_res = grad_out + norm_back(
            grad_two * gain_two.astype(jnp.float32), normed_two, scale_two
        )
        grad_proj = grad_res.astype(jnp.bfloat16)
        d_out_w = jnp.einsum("tj,td->jd", attended, grad_proj, preferred_element_type=jnp.float32)
        grad_att = jnp.einsum(
            "td,jd->tj", grad_proj, weight_o, preferred_element_type=jnp.float32
        ).astype(jnp.bfloat16)
        span_count = batch_index + 1
        gathered = all_keys(jnp.stack(key_store[:span_count], 1))
        positions = (
            batch_index * batch_len + ctx_rank * rows_dev + jnp.arange(rows_dev, dtype=jnp.int32)
        )
        cosine_rows, sine_rows = angles(positions)
        starts = doc_starts[0, batch_index]
        scores = masked_scores(queries, gathered, positions, starts, span_count, batch_len)
        prob_rows = jnp.exp(scores - log_total[..., None])
        weights_low = prob_rows.astype(jnp.bfloat16)
        key_part = gathered[..., :kv_width].reshape(-1, KV_HEADS, HEAD_DIM)
        value_part = gathered[..., kv_width:].reshape(-1, KV_HEADS, HEAD_DIM)
        grad_grouped = grad_att.reshape(rows_dev, KV_HEADS, group_size, HEAD_DIM)
        query_grouped = queries.reshape(rows_dev, KV_HEADS, group_size, HEAD_DIM)
        grad_probs = jnp.einsum(
            "qgcd,jgd->gcqj", grad_grouped, value_part, preferred_element_type=jnp.float32
        )
        grad_scores = (
            prob_rows * (grad_probs - jnp.sum(prob_rows * grad_probs, -1, keepdims=True))
        ).astype(jnp.bfloat16)
        grad_query = (
            jnp.einsum("gcqj,jgd->qgcd", grad_scores, key_part, preferred_element_type=jnp.float32)
            * inverse_root
        )
        grad_key = (
            jnp.einsum(
                "gcqj,qgcd->jgd", grad_scores, query_grouped, preferred_element_type=jnp.float32
            )
            * inverse_root
        )
        grad_value = jnp.einsum(
            "gcqj,qgcd->jgd", weights_low, grad_grouped, preferred_element_type=jnp.float32
        )
        own_terms = lax.psum_scatter(
            jnp.concatenate(
                [
                    grad_key.reshape(rows_dev * lax.axis_size("ctx"), span_count, kv_width),
                    grad_value.reshape(rows_dev * lax.axis_size("ctx"), span_count, kv_width),
                ],
                -1,
            ).astype(jnp.bfloat16),
            "ctx",
            scatter_dimension=0,
            tiled=True,
        ).astype(jnp.float32)
        for earlier in range(span_count):
            key_grads[earlier] = key_grads[earlier] + own_terms[:, earlier]
        own_grads = key_grads[batch_index]
        grad_key_lin = rotate_back(
            own_grads[:, :kv_width].reshape(rows_dev, KV_HEADS, HEAD_DIM), cosine_rows, sine_rows
        )
        grad_key_lin = grad_key_lin.reshape(rows_dev, kv_width).astype(jnp.bfloat16)
        grad_value_in = own_grads[:, kv_width:].astype(jnp.bfloat16)
        grad_query_lin = rotate_back(
            grad_query.reshape(rows_dev, HEADS, HEAD_DIM), cosine_rows, sine_rows
        )
        grad_query_lin = grad_query_lin.reshape(rows_dev, HEADS * HEAD_DIM).astype(jnp.bfloat16)
        d_query_w = jnp.einsum(
            "td,tj->dj", hidden_in, grad_query_lin, preferred_element_type=jnp.float32
        )
        d_key_w = jnp.einsum(
            "td,tj->dj", hidden_in, grad_key_lin, preferred_element_type=jnp.float32
        )
        d_value_w = jnp.einsum(
            "td,tj->dj", hidden_in, grad_value_in, preferred_element_type=jnp.float32
        )
        grad_hidden = jnp.einsum(
            "tj,dj->td", grad_query_lin, weight_q, preferred_element_type=jnp.float32
        )
        grad_hidden = grad_hidden + jnp.einsum(
            "tj,dj->td", grad_key_lin, weight_k, preferred_element_type=jnp.float32
        )
        grad_hidden = grad_hidden + jnp.einsum(
            "tj,dj->td", grad_value_in, weight_v, preferred_element_type=jnp.float32
        )
        inputs = tokens[0, batch_index].astype(jnp.float32)
        normed, scale_rows = normalize(inputs)
        d_gain_one = jnp.sum(grad_hidden * normed, 0)
        input_grads[batch_index] = grad_res + norm_back(
            grad_hidden * gain_one.astype(jnp.float32), normed, scale_rows
        )
        new_terms = (
            d_gain_one,
            d_query_w,
            d_key_w,
            d_value_w,
            d_out_w,
            d_gain_two,
            d_router_w,
            d_gate_w,
            d_up_w,
            d_down_w,
        )
        for position_index in range(10):
            if grad_sums[position_index] is None:
                grad_sums[position_index] = new_terms[position_index]
            else:
                grad_sums[position_index] = grad_sums[position_index] + new_terms[position_index]
    shards = (
        lax.psum_scatter(
            grad_sums[0].astype(jnp.bfloat16), "fsdp", scatter_dimension=0, tiled=True
        ).astype(jnp.float32),
        lax.psum_scatter(
            grad_sums[1].astype(jnp.bfloat16), "fsdp", scatter_dimension=0, tiled=True
        ).astype(jnp.float32),
        lax.psum_scatter(
            grad_sums[2].astype(jnp.bfloat16), "fsdp", scatter_dimension=0, tiled=True
        ).astype(jnp.float32),
        lax.psum_scatter(
            grad_sums[3].astype(jnp.bfloat16), "fsdp", scatter_dimension=0, tiled=True
        ).astype(jnp.float32),
        lax.psum_scatter(
            grad_sums[4].astype(jnp.bfloat16), "fsdp", scatter_dimension=0, tiled=True
        ).astype(jnp.float32),
        lax.psum_scatter(
            grad_sums[5].astype(jnp.bfloat16), "fsdp", scatter_dimension=0, tiled=True
        ).astype(jnp.float32),
        lax.psum_scatter(
            grad_sums[6].astype(jnp.bfloat16), "fsdp", scatter_dimension=0, tiled=True
        ).astype(jnp.float32),
        lax.psum_scatter(
            grad_sums[7].astype(jnp.bfloat16), "fsdp", scatter_dimension=1, tiled=True
        ).astype(jnp.float32),
        lax.psum_scatter(
            grad_sums[8].astype(jnp.bfloat16), "fsdp", scatter_dimension=1, tiled=True
        ).astype(jnp.float32),
        lax.psum_scatter(
            grad_sums[9].astype(jnp.bfloat16), "fsdp", scatter_dimension=1, tiled=True
        ).astype(jnp.float32),
    )
    dense_grads = (
        lax.psum(shards[0].astype(jnp.bfloat16), "ctx").astype(jnp.float32),
        lax.psum(shards[1].astype(jnp.bfloat16), "ctx").astype(jnp.float32),
        lax.psum(shards[2].astype(jnp.bfloat16), "ctx").astype(jnp.float32),
        lax.psum(shards[3].astype(jnp.bfloat16), "ctx").astype(jnp.float32),
        lax.psum(shards[4].astype(jnp.bfloat16), "ctx").astype(jnp.float32),
        lax.psum(shards[5].astype(jnp.bfloat16), "ctx").astype(jnp.float32),
        lax.psum(shards[6].astype(jnp.bfloat16), "ctx").astype(jnp.float32),
    )
    mixed = jnp.stack(mixed_parts, 0)[None]
    d_tokens = jnp.stack(input_grads, 0)[None]
    return (
        mixed,
        d_tokens,
        dense_grads[0],
        dense_grads[1],
        dense_grads[2],
        dense_grads[3],
        dense_grads[4],
        dense_grads[5],
        dense_grads[6],
        shards[7],
        shards[8],
        shards[9],
    )


def solution(mesh):
    return jax.shard_map(
        per_device,
        mesh=mesh,
        in_specs=(
            P("fsdp", None, "ctx", None),
            P("fsdp", None, "ctx", None),
            P("fsdp", None, "ctx"),
            P("fsdp"),
            P("fsdp", None),
            P("fsdp", None),
            P("fsdp", None),
            P("fsdp", None),
            P("fsdp"),
            P("fsdp", None),
            P("ctx", "fsdp", None),
            P("ctx", "fsdp", None),
            P("ctx", "fsdp", None),
            P("fsdp", None, "ctx", None),
        ),
        out_specs=(
            P("fsdp", None, "ctx", None),
            P("fsdp", None, "ctx", None),
            P("fsdp"),
            P("fsdp", None),
            P("fsdp", None),
            P("fsdp", None),
            P("fsdp", None),
            P("fsdp"),
            P("fsdp", None),
            P("ctx", "fsdp", None),
            P("ctx", "fsdp", None),
            P("ctx", "fsdp", None),
        ),
        check_vma=False,
    )
```

profile of v0, /device:TPU:0, one launch (start us, length us, event | category | flops | bytes accessed | tf_op | source)
XLA Modules:
  0.0 1657.5 jit_solution(6045283919362985270)
XLA Ops:
  13.1 41.0 %all-reduce.7 = (bf16[1024]{0:T(1024)(128)(2,1)S(1)}, bf16[1024]{0:T(1024)(128)(2,1)S(1)}) all-reduce(bf16[1024]{0:T(1024)(128)(2,1)S(1)} %dynamic-update-slice, bf16[1024]{0:T(1024)(128)(2,1)S(1)} %dynamic-update-slice.1), channel_id=1, replica_groups=mesh['ctx'=8,'fsdp'=16] {'fsdp'}, use_global_device_ids=true, to_apply=%add | all-reduce | flops 2048 | bytes 8192
  58.4 40.9 %all-gather.14.cloned.1.call-done = bf16[1024,512]{1,0:T(8,128)(2,1)} async-done(((bf16[64,512]{1,0:T(8,128)(2,1)}), bf16[1024,512]{1,0:T(8,128)(2,1)}) %all-gather.14.cloned.1.call-update) | async-done | bytes 1048592 | tf_op jit(solution)/shard_map/all_gather | solution.py:111
  122.1 23.5 %all-gather.16.cloned.1.call-done = bf16[1024,1024]{1,0:T(8,128)(2,1)} async-done(((bf16[64,1024]{1,0:T(8,128)(2,1)}), bf16[1024,1024]{1,0:T(8,128)(2,1)}) %all-gather.16.cloned.1.call-update) | async-done | bytes 2097168 | tf_op jit(solution)/shard_map/all_gather | solution.py:109
  149.4 23.2 %all-gather.28.cloned.1.call-done = bf16[1024,1024]{1,0:T(8,128)(2,1)} async-done(((bf16[128,1024]{1,0:T(8,128)(2,1)}), bf16[1024,1024]{1,0:T(8,128)(2,1)}) %all-gather.28.cloned.1.call-update) | async-done | bytes 2097168 | tf_op jit(solution)/shard_map/all_gather | solution.py:121
  185.2 34.5 %all-gather.18.cloned.1.call-done = bf16[1024,1024]{1,0:T(8,128)(2,1)} async-done(((bf16[64,1024]{1,0:T(8,128)(2,1)}), bf16[1024,1024]{1,0:T(8,128)(2,1)}) %all-gather.18.cloned.1.call-update) | async-done | bytes 2097168 | tf_op jit(solution)/shard_map/all_gather | solution.py:112
  236.7 15.7 reduce-window.16
  257.2 23.0 %all-gather.1 = bf16[16,64,32]{1,2,0:T(8,128)(2,1)S(1)} all-gather(bf16[1,64,32]{1,2,0:T(8,128)(2,1)} %bitcast.703), channel_id=1, replica_groups=mesh['ctx'=8,'fsdp'=16] {'fsdp'}, dimensions={0}, use_global_device_ids=true | all-gather | bytes 69632 | tf_op jit(solution)/shard_map/all_gather | solution.py:114
  287.3 38.9 %all-gather.22.cloned.1.call-done = bf16[4,1024,512]{2,1,0:T(8,128)(2,1)} async-done(((bf16[4,64,512]{2,1,0:T(8,128)(2,1)}), bf16[4,1024,512]{2,1,0:T(8,128)(2,1)}) %all-gather.22.cloned.1.call-update) | async-done | bytes 4194320 | tf_op jit(solution)/shard_map/all_gather | solution.py:116
  332.9 46.6 %all-gather.24.cloned.1.call-done = bf16[4,512,1024]{2,1,0:T(8,128)(2,1)} async-done(((bf16[4,32,1024]{2,1,0:T(8,128)(2,1)}), bf16[4,512,1024]{2,1,0:T(8,128)(2,1)}) %all-gather.24.cloned.1.call-update) | async-done | bytes 4194320 | tf_op jit(solution)/shard_map/all_gather | solution.py:117
  413.5 26.2 %all-to-all-done.1 = bf16[8,4,40,1024]{3,2,1,0:T(8,128)(2,1)S(1)} async-done(((bf16[8,4,40,1024]{3,2,1,0:T(8,128)(2,1)}), bf16[8,4,40,1024]{3,2,1,0:T(8,128)(2,1)S(1)}, u32[]{:S(2)}, u32[]{:S(2)}) %all-to-all-start.1) | async-done | bytes 2621472 | tf_op jit(solution)/shard_map/all_to_all | solution.py:127
  552.1 36.3 %all_to_all.40 = bf16[8,4,40,1024]{3,2,1,0:T(8,128)(2,1)S(1)} all-to-all(bf16[8,4,40,1024]{3,2,1,0:T(8,128)(2,1)S(1)} %bitcast.640), channel_id=1, replica_groups=mesh['ctx'=8,'fsdp'=16] {'ctx'}, dimensions={0} | all-to-all | bytes 5242880 | tf_op jit(solution)/shard_map/all_to_all | solution.py:124
  617.8 17.8 %all-to-all-done.3 = bf16[8,4,40,1024]{3,2,1,0:T(8,128)(2,1)S(1)} async-done(((bf16[8,4,40,1024]{3,2,1,0:T(8,128)(2,1)}), bf16[8,4,40,1024]{3,2,1,0:T(8,128)(2,1)S(1)}, u32[]{:S(2)}, u32[]{:S(2)}) %all-to-all-start.3) | async-done | bytes 2621472 | tf_op jit(solution)/shard_map/all_to_all | solution.py:127
  654.5 36.3 %all_to_all.41 = bf16[8,4,40,1024]{3,2,1,0:T(8,128)(2,1)S(1)} all-to-all(bf16[8,4,40,1024]{3,2,1,0:T(8,128)(2,1)S(1)} %bitcast.639), channel_id=1, replica_groups=mesh['ctx'=8,'fsdp'=16] {'ctx'}, dimensions={0} | all-to-all | bytes 5242880 | tf_op jit(solution)/shard_map/all_to_all | solution.py:124
  712.0 26.8 %all-to-all-done.7 = bf16[8,4,40,1024]{3,2,1,0:T(8,128)(2,1)S(1)} async-done(((bf16[8,4,40,1024]{3,2,1,0:T(8,128)(2,1)}), bf16[8,4,40,1024]{3,2,1,0:T(8,128)(2,1)S(1)}, u32[]{:S(2)}, u32[]{:S(2)}) %all-to-all-start.7) | async-done | bytes 2621472 | tf_op jit(solution)/shard_map/all_to_all | solution.py:127
  881.4 83.5 %all-reduce.16.cloned.1.call-done = (bf16[1024,2,1024]{2,1,0:T(2,128)(2,1)}, bf16[1024,1,1024]{2,1,0:T(2,128)(2,1)}) async-done(((bf16[1024,2,1024]{2,1,0:T(2,128)(2,1)}, bf16[1024,1,1024]{2,1,0:T(2,128)(2,1)}), (bf16[1024,2,1024]{2,1,0:T(2,128)(2,1)}, bf16[1024,1,1024]{2,1,0:T(2,128)(2,1)})) %all-reduce.16.cloned.1.call-update) | async-done | bytes 6291472
  982.6 59.4 %reduce-scatter.17.cloned.1.call-done = bf16[64,1024]{1,0:T(8,128)(2,1)} async-done(((bf16[1024,1024]{1,0:T(8,128)(2,1)}), bf16[64,1024]{1,0:T(8,128)(2,1)}) %reduce-scatter.17.cloned.1.call-update) | async-done | bytes 131088 | tf_op jit(solution)/shard_map/reduce_scatter | solution.py:422
  1042.1 77.0 %reduce-scatter.11.cloned.1.call-done = bf16[64,1024]{1,0:T(8,128)(2,1)} async-done(((bf16[1024,1024]{1,0:T(8,128)(2,1)}), bf16[64,1024]{1,0:T(8,128)(2,1)}) %reduce-scatter.11.cloned.1.call-update) | async-done | bytes 131088 | tf_op jit(solution)/shard_map/reduce_scatter | solution.py:413
  1119.1 75.3 %reduce-scatter.15.cloned.1.call-done = bf16[64,512]{1,0:T(8,128)(2,1)} async-done(((bf16[1024,512]{1,0:T(8,128)(2,1)}), bf16[64,512]{1,0:T(8,128)(2,1)}) %reduce-scatter.15.cloned.1.call-update) | async-done | bytes 65552 | tf_op jit(solution)/shard_map/reduce_scatter | solution.py:419
  1194.4 76.2 %reduce-scatter.13.cloned.1.call-done = bf16[64,512]{1,0:T(8,128)(2,1)} async-done(((bf16[1024,512]{1,0:T(8,128)(2,1)}), bf16[64,512]{1,0:T(8,128)(2,1)}) %reduce-scatter.13.cloned.1.call-update) | async-done | bytes 65552 | tf_op jit(solution)/shard_map/reduce_scatter | solution.py:416
  1298.9 46.6 %reduce-scatter.25.cloned.1.call-done = bf16[64,32]{1,0:T(8,128)(2,1)} async-done(((bf16[1024,32]{1,0:T(8,128)(2,1)}), bf16[64,32]{1,0:T(8,128)(2,1)}) %reduce-scatter.25.cloned.1.call-update) | async-done | bytes 4112
  1353.1 38.1 %all-reduce.6 = (bf16[1024]{0:T(1024)(128)(2,1)S(1)}, bf16[1024]{0:T(1024)(128)(2,1)S(1)}) all-reduce(bf16[1024]{0:T(1024)(128)(2,1)S(1)} %add_convert_fusion.11, bf16[1024]{0:T(1024)(128)(2,1)S(1)} %add_convert_fusion.10), channel_id=5, replica_groups=mesh['ctx'=8,'fsdp'=16] {'fsdp'}, use_global_device_ids=true, to_apply=%region_34.36.clone | all-reduce | flops 2048 | bytes 8192
  1414.7 73.5 %reduce-scatter.23.cloned.1.call-done = bf16[4,32,1024]{2,1,0:T(8,128)(2,1)} async-done(((bf16[4,512,1024]{2,1,0:T(8,128)(2,1)}), bf16[4,32,1024]{2,1,0:T(8,128)(2,1)}) %reduce-scatter.23.cloned.1.call-update) | async-done | bytes 262160 | tf_op jit(solution)/shard_map/reduce_scatter | solution.py:437
  1490.0 78.7 %reduce-scatter.19.cloned.1.call-done = bf16[4,64,512]{2,1,0:T(8,128)(2,1)} async-done(((bf16[4,1024,512]{2,1,0:T(8,128)(2,1)}), bf16[4,64,512]{2,1,0:T(8,128)(2,1)}) %reduce-scatter.19.cloned.1.call-update) | async-done | bytes 262160 | tf_op jit(solution)/shard_map/reduce_scatter | solution.py:431
  1570.5 78.4 %reduce-scatter.21.cloned.1.call-done = bf16[4,64,512]{2,1,0:T(8,128)(2,1)} async-done(((bf16[4,1024,512]{2,1,0:T(8,128)(2,1)}), bf16[4,64,512]{2,1,0:T(8,128)(2,1)}) %reduce-scatter.21.cloned.1.call-update) | async-done | bytes 262160 | tf_op jit(solution)/shard_map/reduce_scatter | solution.py:434
  (575 shorter events, 521.8 us)
Async XLA Ops:
  7.2 49.0 %all-gather.12.cloned.1.call-start = ((), (), s32[]{:S(2)}) async-start(), calls=%async_computation.16 | async-start | bytes 1114112 | tf_op jit(solution)/shard_map/all_gather | solution.py:110
  7.9 91.4 %all-gather.14.cloned.1.call-start = ((), (), s32[]{:S(2)}) async-start(), calls=%async_computation.17 | async-start | bytes 1114112 | tf_op jit(solution)/shard_map/all_gather | solution.py:111
  8.7 136.9 %all-gather.16.cloned.1.call-start = ((), (), s32[]{:S(2)}) async-start(), calls=%async_computation.18 | async-start | bytes 2228224 | tf_op jit(solution)/shard_map/all_gather | solution.py:109
  9.4 163.1 %all-gather.28.cloned.1.call-start = ((), (), s32[]{:S(2)}) async-start(), calls=%async_computation.31 | async-start | bytes 2359296 | tf_op jit(solution)/shard_map/all_gather | solution.py:121
  101.7 117.9 %all-gather.18.cloned.1.call-start = ((), (), s32[]{:S(2)}) async-start(), calls=%async_computation.19 | async-start | bytes 2228224 | tf_op jit(solution)/shard_map/all_gather | solution.py:112
  102.3 178.7 %all-gather.20.cloned.1.call-start = ((), (), s32[]{:S(2)}) async-start(), calls=%async_computation.20 | async-start | bytes 4456448 | tf_op jit(solution)/shard_map/all_gather | solution.py:115
  102.9 223.2 %all-gather.22.cloned.1.call-start = ((), (), s32[]{:S(2)}) async-start(), calls=%async_computation.21 | async-start | bytes 4456448 | tf_op jit(solution)/shard_map/all_gather | solution.py:116
  103.7 275.9 %all-gather.24.cloned.1.call-start = ((), (), s32[]{:S(2)}) async-start(), calls=%async_computation.22 | async-start | bytes 4456448 | tf_op jit(solution)/shard_map/all_gather | solution.py:117
  225.8 55.2 %all-to-all-start = ((bf16[8,4,40,1024]{3,2,1,0:T(8,128)(2,1)}), bf16[8,4,40,1024]{3,2,1,0:T(8,128)(2,1)S(1)}, u32[]{:S(2)}, u32[]{:S(2)}) async-start(bf16[8,4,40,1024]{3,2,1,0:T(8,128)(2,1)} %bitcast.636), calls=%async_computation | async-start | bytes 5242880 | tf_op jit(solution)/shard_map/all_to_all | solution.py:124
  230.5 234.4 %all-gather.26.cloned.1.call-start = ((), (), s32[]{:S(2)}) async-start(), calls=%async_computation.23 | async-start | bytes 4718592 | tf_op jit(solution)/shard_map/all_gather | solution.py:121
  385.4 54.2 %all-to-all-start.1 = ((bf16[8,4,40,1024]{3,2,1,0:T(8,128)(2,1)}), bf16[8,4,40,1024]{3,2,1,0:T(8,128)(2,1)S(1)}, u32[]{:S(2)}, u32[]{:S(2)}) async-start(bf16[8,4,40,1024]{3,2,1,0:T(8,128)(2,1)} %copy.165), calls=%async_computation.1 | async-start | bytes 5242880 | tf_op jit(solution)/shard_map/all_to_all | solution.py:127
  460.1 37.6 %all-to-all-start.4 = ((bf16[8,4,40,1024]{3,2,1,0:T(8,128)(2,1)}), bf16[8,4,40,1024]{3,2,1,0:T(8,128)(2,1)}, u32[]{:S(2)}, u32[]{:S(2)}) async-start(bf16[8,4,40,1024]{3,2,1,0:T(8,128)(2,1)} %bitcast.80), calls=%async_computation.4 | async-start | bytes 5242880 | tf_op jit(solution)/shard_map/all_to_all | solution.py:124
  510.4 36.5 %all-to-all-start.5 = ((bf16[8,4,40,1024]{3,2,1,0:T(8,128)(2,1)}), bf16[8,4,40,1024]{3,2,1,0:T(8,128)(2,1)S(1)}, u32[]{:S(2)}, u32[]{:S(2)}) async-start(bf16[8,4,40,1024]{3,2,1,0:T(8,128)(2,1)} %copy.181), calls=%async_computation.5 | async-start | bytes 5242880 | tf_op jit(solution)/shard_map/all_to_all | solution.py:127
  599.1 36.5 %all-to-all-start.3 = ((bf16[8,4,40,1024]{3,2,1,0:T(8,128)(2,1)}), bf16[8,4,40,1024]{3,2,1,0:T(8,128)(2,1)S(1)}, u32[]{:S(2)}, u32[]{:S(2)}) async-start(bf16[8,4,40,1024]{3,2,1,0:T(8,128)(2,1)} %copy.178), calls=%async_computation.3 | async-start | bytes 5242880 | tf_op jit(solution)/shard_map/all_to_all | solution.py:127
  706.1 258.9 %all-reduce.16.cloned.1.call-start = ((), (), s32[]{:S(2)}) async-start(), calls=%async_computation.34 | async-start | bytes 16777216
  862.6 179.5 %reduce-scatter.17.cloned.1.call-start = ((), (), s32[]{:S(2)}) async-start(), calls=%async_computation.27 | async-start | bytes 2228224 | tf_op jit(solution)/shard_map/reduce_scatter | solution.py:422
  866.5 252.6 %reduce-scatter.11.cloned.1.call-start = ((), (), s32[]{:S(2)}) async-start(), calls=%async_computation.24 | async-start | bytes 2228224 | tf_op jit(solution)/shard_map/reduce_scatter | solution.py:413
  880.2 314.2 %reduce-scatter.15.cloned.1.call-start = ((), (), s32[]{:S(2)}) async-start(), calls=%async_computation.26 | async-start | bytes 1114112 | tf_op jit(solution)/shard_map/reduce_scatter | solution.py:419
  970.8 299.8 %reduce-scatter.13.cloned.1.call-start = ((), (), s32[]{:S(2)}) async-start(), calls=%async_computation.25 | async-start | bytes 1114112 | tf_op jit(solution)/shard_map/reduce_scatter | solution.py:416
  973.5 372.0 %reduce-scatter.25.cloned.1.call-start = ((), (), s32[]{:S(2)}) async-start(), calls=%async_computation.32 | async-start | bytes 278528
  975.0 433.4 %all-reduce.14.cloned.1.call-start = ((), (), s32[]{:S(2)}) async-start(), calls=%async_computation.33 | async-start | bytes 786432 | tf_op jit(solution)/shard_map/psum | solution.py:443
  1270.6 217.6 %reduce-scatter.23.cloned.1.call-start = ((), (), s32[]{:S(2)}) async-start(), calls=%async_computation.30 | async-start | bytes 4456448 | tf_op jit(solution)/shard_map/reduce_scatter | solution.py:437
  1279.5 289.2 %reduce-scatter.19.cloned.1.call-start = ((), (), s32[]{:S(2)}) async-start(), calls=%async_computation.28 | async-start | bytes 4456448 | tf_op jit(solution)/shard_map/reduce_scatter | solution.py:431
  1288.7 360.2 %reduce-scatter.21.cloned.1.call-start = ((), (), s32[]{:S(2)}) async-start(), calls=%async_computation.29 | async-start | bytes 4456448 | tf_op jit(solution)/shard_map/reduce_scatter | solution.py:434
  (140 other events, 3761.8 us)
Sparse Core Ops, SparseCore 0:
  10.2 45.0 all-gather.11
  57.4 41.8 all-gather.13
  101.4 44.0 all-gather.15
  147.7 24.7 all-gather.27
  174.5 45.1 all-gather.17
  221.7 51.0 all-gather.19
  274.9 51.1 all-gather.21
  328.3 51.1 all-gather.23
  381.8 51.3 all-gather.25
  862.7 102.1 all-reduce.15
  968.2 73.8 reduce-scatter.16
  1045.5 73.4 reduce-scatter.10
  1122.3 72.0 reduce-scatter.14
  1198.4 72.1 reduce-scatter.12
  1274.1 71.3 reduce-scatter.24
  1348.1 60.2 all-reduce.13
  1411.5 76.6 reduce-scatter.22
  1491.8 76.8 reduce-scatter.18
  1572.0 76.8 reduce-scatter.20
where the time goes:
time: 1660 us
  waiting for transfers between devices  935 us (56%)
  matrix products  200 us (12%)
  blocking collectives  188 us (11%)
  local copies, waits for them, and re-layouts  148 us (9%)
  other arithmetic  141 us (8%)
  starting transfers between devices  27.4 us (2%)
  between operations  18.5 us (1%)
    unnamed x21, waiting for transfers between devices  134 us
    unnamed x2, blocking collectives  79.1 us
    reduce_scatter x1, waiting for transfers between devices, per_device(): lax.psum_scatter(grad_sums[7].astype(jnp.bfloat16), 'fsdp', scatter_dimen...  78.7 us
    reduce_scatter x1, waiting for transfers between devices, per_device(): lax.psum_scatter(grad_sums[8].astype(jnp.bfloat16), 'fsdp', scatter_dimen...  78.4 us
    reduce_scatter x1, waiting for transfers between devices, per_device(): lax.psum_scatter(grad_sums[1].astype(jnp.bfloat16), 'fsdp', scatter_dimen...  77 us
    reduce_scatter x1, waiting for transfers between devices, per_device(): lax.psum_scatter(grad_sums[2].astype(jnp.bfloat16), 'fsdp', scatter_dimen...  76.2 us
    reduce_scatter x1, waiting for transfers between devices, per_device(): lax.psum_scatter(grad_sums[3].astype(jnp.bfloat16), 'fsdp', scatter_dimen...  75.3 us
    reduce_scatter x1, waiting for transfers between devices, per_device(): lax.psum_scatter(grad_sums[9].astype(jnp.bfloat16), 'fsdp', scatter_dimen...  73.5 us
  transfers between devices with their start and end apart: 25, of which 20 were waited for; matrix products, arithmetic and copies ran while one was open for 18% of the time, Pallas kernels for 0%

commit v1 on v0

v1 whole, which is shorter than its diff:
```python
import functools
import math

import jax
import jax.numpy as jnp
from jax import lax
from jax.experimental import pallas as pl
from jax.experimental.pallas import tpu as pltpu
from jax.sharding import PartitionSpec as P

HEADS = 16
KV_HEADS = 8
HEAD_DIM = 64
MICRO = 2
EPSILON = 1e-06
HIDDEN = -1e30
BF = jnp.bfloat16
F32 = jnp.float32
HIGHEST = lax.Precision.HIGHEST
PAIR = 2 * HEAD_DIM
VMEM_LIMIT = 56 * 1024 * 1024

NN = (((1,), (0,)), ((), ()))
NT = (((1,), (1,)), ((), ()))
TN = (((0,), (0,)), ((), ()))


def mm(left, right, dims=NN, precision=None):
    return lax.dot_general(left, right, dims, preferred_element_type=F32, precision=precision)


def params():
    return pltpu.CompilerParams(vmem_limit_bytes=VMEM_LIMIT)


def cost(flops, moved):
    return pl.CostEstimate(flops=int(flops), bytes_accessed=int(moved), transcendentals=0)


def lanes(shape):
    return lax.broadcasted_iota(jnp.int32, shape, len(shape) - 1)


def turn(values, cosine, sine):
    spot = lanes(values.shape) % HEAD_DIM
    swapped = jnp.where(
        spot < HEAD_DIM // 2,
        pltpu.roll(values, PAIR - HEAD_DIM // 2, 1),
        pltpu.roll(values, HEAD_DIM // 2, 1),
    )
    return values * cosine + swapped * sine


def angle_tables(length):
    half = HEAD_DIM // 2
    frequencies = 10000.0 ** (-2.0 * jnp.arange(half, dtype=F32) / HEAD_DIM)
    turned = jnp.arange(length, dtype=jnp.int32).astype(F32)[:, None] * frequencies[None, :]
    cosine, sine = jnp.cos(turned), jnp.sin(turned)
    return (
        jnp.concatenate([cosine] * 4, -1),
        jnp.concatenate([-sine, sine, -sine, sine], -1),
    )


def project_kernel(x_ref, w_ref, gain_ref, cos_ref, sin_ref, q_ref, kv_ref, h_ref):
    rows = x_ref.shape[1]
    x = x_ref[0].astype(F32)
    scale = lax.rsqrt(jnp.mean(x * x, -1, keepdims=True) + EPSILON)
    h = (x * scale * gain_ref[...]).astype(BF)
    h_ref[0] = h
    lin = mm(h, w_ref[...])
    cosine = cos_ref[...].reshape(rows, PAIR)
    sine = sin_ref[...].reshape(rows, PAIR)
    q = turn(lin[:, :PAIR], cosine, sine).astype(BF).astype(F32)
    q_ref[...] = (q * (1.0 / math.sqrt(HEAD_DIM))).astype(BF).reshape(q_ref.shape)
    flat = lin[:, PAIR:]
    kv = jnp.where(lanes(flat.shape) < HEAD_DIM, turn(flat, cosine, sine), flat)
    kv_ref[...] = kv.astype(BF).reshape(kv_ref.shape)


def project(x_all, weight, gain, cosine, sine):
    units, rows, width = x_all.shape
    length = units * rows // MICRO
    part = rows // MICRO
    place = pl.BlockSpec((MICRO, part, PAIR), lambda u: (0, u, 0))
    table = pl.BlockSpec((MICRO, part, PAIR), lambda u: (0, u, 0))
    return pl.pallas_call(
        project_kernel,
        grid=(units,),
        in_specs=[
            pl.BlockSpec((1, rows, width), lambda u: (u, 0, 0)),
            pl.BlockSpec((width, 2 * PAIR), lambda u: (0, 0)),
            pl.BlockSpec((1, width), lambda u: (0, 0)),
            table,
            table,
        ],
        out_specs=[place, place, pl.BlockSpec((1, rows, width), lambda u: (u, 0, 0))],
        out_shape=[
            jax.ShapeDtypeStruct((MICRO, length, PAIR), BF),
            jax.ShapeDtypeStruct((MICRO, length, PAIR), BF),
            jax.ShapeDtypeStruct((units, rows, width), BF),
        ],
        compiler_params=params(),
        cost_estimate=cost(2 * units * rows * width * 2 * PAIR, 4 * units * rows * width),
        name="project",
    )(
        x_all,
        weight,
        gain,
        cosine.reshape(MICRO, length, PAIR),
        sine.reshape(MICRO, length, PAIR),
    )


def front_heads(pair):
    pair = pair.astype(F32)
    front = lanes(pair.shape) < HEAD_DIM
    return jnp.concatenate(
        [jnp.where(front, pair, 0.0), jnp.where(front, pltpu.roll(pair, HEAD_DIM, 1), 0.0)], 0
    ).astype(BF)


def back_heads(pair):
    pair = pair.astype(F32)
    back = lanes(pair.shape) >= HEAD_DIM
    return jnp.concatenate(
        [jnp.where(back, pltpu.roll(pair, HEAD_DIM, 1), 0.0), jnp.where(back, pair, 0.0)], 0
    ).astype(BF)


def attend_kernel(q_ref, kv_ref, start_ref, o_ref, lse_ref, s_ref, kvt_ref, acc_ref):
    tile = pl.program_id(0)
    rows = q_ref.shape[0]
    chunks = kv_ref.shape[0]

    @pl.when(tile == 0)
    def _():
        for chunk in range(chunks):
            kvt_ref[chunk] = kv_ref[chunk].astype(F32).T.astype(BF)

    queries = front_heads(q_ref[...])
    start = jnp.concatenate([start_ref[0], start_ref[0]], -1)
    key_row = lax.broadcasted_iota(jnp.int32, (rows, 2 * rows), 0)
    query_row = lanes((rows, 2 * rows)) % rows

    def scores(chunk):
        found = mm(kv_ref[chunk], queries, NT)
        return jnp.where(key_row >= start - chunk * rows, found, HIDDEN)

    def fold(values, how):
        return how(values.reshape(rows // 8, 8, 2 * rows), axis=0)

    def fill(chunk, top):
        found = scores(chunk)
        s_ref[chunk] = found
        return jnp.maximum(top, fold(found, jnp.max))

    own = jnp.where(key_row <= query_row, scores(tile), HIDDEN)
    s_ref[tile] = own
    top = lax.fori_loop(0, tile, fill, fold(own, jnp.max))
    top = jnp.max(top, axis=0, keepdims=True)
    acc_ref[...] = jnp.zeros_like(acc_ref)

    def weigh(chunk, total):
        raised = jnp.exp(s_ref[chunk] - top)
        acc_ref[...] += mm(kvt_ref[chunk], raised.astype(BF))
        return total + fold(raised, jnp.sum)

    total = lax.fori_loop(0, tile + 1, weigh, jnp.zeros((8, 2 * rows), F32))
    total = jnp.sum(total, axis=0, keepdims=True)
    out = acc_ref[HEAD_DIM:, :] * (1.0 / total)
    out = jnp.concatenate([out[:, :rows], out[:, rows:]], 0)
    o_ref[...] = out.T.astype(BF)
    lse_ref[0] = top + jnp.log(total)


def attend(q, kv, starts, rows=256):
    length = q.shape[0]
    tiles = length // rows
    return pl.pallas_call(
        attend_kernel,
        grid=(tiles,),
        in_specs=[
            pl.BlockSpec((rows, PAIR), lambda t: (t, 0)),
            pl.BlockSpec((tiles, rows, PAIR), lambda t: (0, 0, 0)),
            pl.BlockSpec((1, 1, rows), lambda t: (t, 0, 0)),
        ],
        out_specs=[
            pl.BlockSpec((rows, PAIR), lambda t: (t, 0)),
            pl.BlockSpec((1, 1, 2 * rows), lambda t: (t, 0, 0)),
        ],
        out_shape=[
            jax.ShapeDtypeStruct((length, PAIR), BF),
            jax.ShapeDtypeStruct((tiles, 1, 2 * rows), F32),
        ],
        scratch_shapes=[
            pltpu.VMEM((tiles, rows, 2 * rows), F32),
            pltpu.VMEM((tiles, PAIR, rows), BF),
            pltpu.VMEM((PAIR, 2 * rows), F32),
        ],
        compiler_params=params(),
        cost_estimate=cost(8 * length * length * PAIR, 8 * length * PAIR),
        name="attend",
    )(q, kv.reshape(tiles, rows, PAIR), starts.reshape(tiles, 1, rows))


def attend_back_kernel(
    q_ref, kv_ref, start_ref, lse_ref, o_ref, do_ref, cos_ref, sin_ref, dq_ref, dkv_ref,
    kvt_ref, dkv_acc, dq_acc,
):
    tile = pl.program_id(0)
    rows = q_ref.shape[0]
    chunks = kv_ref.shape[0]

    @pl.when(tile == 0)
    def _():
        dkv_acc[...] = jnp.zeros_like(dkv_acc)
        for chunk in range(chunks):
            kvt_ref[chunk] = kv_ref[chunk].astype(F32).T.astype(BF)

    grad_o = do_ref[...].reshape(rows, PAIR)
    queries = front_heads(q_ref[...])
    grads = back_heads(grad_o)
    product = grad_o.astype(F32) * o_ref[...].astype(F32)
    half = lax.broadcasted_iota(jnp.int32, (8, PAIR), 0)
    picked = (lanes((8, PAIR)) // HEAD_DIM == half).astype(F32)
    sums = mm(picked, product, NT, HIGHEST)
    delta = jnp.concatenate([sums[0:1], sums[1:2]], -1)
    start = jnp.concatenate([start_ref[0], start_ref[0]], -1)
    lse = lse_ref[0]
    key_row = lax.broadcasted_iota(jnp.int32, (rows, 2 * rows), 0)
    query_row = lanes((rows, 2 * rows)) % rows
    dq_acc[...] = jnp.zeros_like(dq_acc)

    def step(chunk, causal):
        keys = kv_ref[chunk]
        seen = key_row >= start - chunk * rows
        if causal:
            seen = seen & (key_row <= query_row)
        found = jnp.where(seen, mm(keys, queries, NT), HIDDEN)
        prob = jnp.exp(found - lse)
        grad_s = (prob * (mm(keys, grads, NT) - delta)).astype(BF)
        dkv_acc[chunk] += mm(grad_s, queries) + mm(prob.astype(BF), grads)
        dq_acc[...] += mm(kvt_ref[chunk], grad_s)

    def earlier(chunk, carry):
        step(chunk, False)
        return carry

    lax.fori_loop(0, tile, earlier, 0)
    step(tile, True)
    dq = dq_acc[:HEAD_DIM, :] * (1.0 / math.sqrt(HEAD_DIM))
    dq = jnp.concatenate([dq[:, :rows], dq[:, rows:]], 0).T
    mine = pl.ds(pl.multiple_of(tile * rows, rows), rows)
    dq_ref[...] = turn(dq, cos_ref[mine, :], -sin_ref[mine, :]).astype(BF)

    @pl.when(tile == chunks - 1)
    def _():
        for chunk in range(chunks):
            flat = dkv_acc[chunk]
            spot = pl.ds(chunk * rows, rows)
            turned = turn(flat, cos_ref[spot, :], -sin_ref[spot, :])
            dkv_ref[spot, :] = jnp.where(lanes(flat.shape) < HEAD_DIM, turned, flat).astype(BF)


def attend_back(q, kv, starts, lse, o, grad_o, cosine, sine, rows=256):
    length = q.shape[0]
    tiles = length // rows
    units, _, part, _ = grad_o.shape
    span = rows // part
    half = tiles // MICRO
    whole = pl.BlockSpec((length, PAIR), lambda t: (0, 0))
    return pl.pallas_call(
        attend_back_kernel,
        grid=(tiles,),
        in_specs=[
            pl.BlockSpec((rows, PAIR), lambda t: (t, 0)),
            pl.BlockSpec((tiles, rows, PAIR), lambda t: (0, 0, 0)),
            pl.BlockSpec((1, 1, rows), lambda t: (t, 0, 0)),
            pl.BlockSpec((1, 1, 2 * rows), lambda t: (t, 0, 0)),
            pl.BlockSpec((rows, PAIR), lambda t: (t, 0)),
            pl.BlockSpec((span, 1, part, PAIR), lambda t: (t % half, t // half, 0, 0)),
            whole,
            whole,
        ],
        out_specs=[pl.BlockSpec((rows, PAIR), lambda t: (t, 0)), whole],
        out_shape=[
            jax.ShapeDtypeStruct((length, PAIR), BF),
            jax.ShapeDtypeStruct((length, PAIR), BF),
        ],
        scratch_shapes=[
            pltpu.VMEM((tiles, PAIR, rows), BF),
            pltpu.VMEM((tiles, rows, PAIR), F32),
            pltpu.VMEM((PAIR, 2 * rows), F32),
        ],
        compiler_params=params(),
        cost_estimate=cost(20 * length * length * PAIR, 16 * length * PAIR),
        name="attend_back",
    )(q, kv.reshape(tiles, rows, PAIR), starts.reshape(tiles, 1, rows), lse, o, grad_o, cosine, sine)


def one_hot(rank_rows, local, capacity):
    slots = lax.broadcasted_iota(jnp.int32, (capacity, rank_rows.shape[1]), 0).astype(F32)
    return jnp.concatenate([(rank_rows[e : e + 1] == slots).astype(F32) for e in range(local)], 0)


def route_kernel(
    local, capacity,
    own_ref, o_ref, x_ref, g_ref, wo_ref, gain_ref, router_ref, routes_ref,
    xs_ref, gs_ref, slot_gate_ref, rank_ref, x1_ref, h2_ref, gates_ref,
):
    unit = pl.program_id(0)
    rows = x_ref.shape[1]
    experts = router_ref.shape[0]
    groups = o_ref.shape[0]
    heads = jnp.concatenate([o_ref[i].reshape(rows, PAIR) for i in range(groups)], 1)
    x1 = x_ref[0].astype(F32) + mm(heads, wo_ref[...])
    scale = lax.rsqrt(jnp.mean(x1 * x1, -1, keepdims=True) + EPSILON)
    h2 = (x1 * scale * gain_ref[...]).astype(BF)
    logits = mm(router_ref[...], h2, NT)
    ids = lax.broadcasted_iota(jnp.int32, (experts, rows), 0)
    chosen = jnp.zeros((experts, rows), F32)
    for k in range(routes_ref.shape[1]):
        chosen = chosen + (ids == routes_ref[0, k : k + 1, :]).astype(F32)
    masked = jnp.where(chosen > 0, logits, HIDDEN)
    raised = jnp.where(chosen > 0, jnp.exp(masked - jnp.max(masked, 0, keepdims=True)), 0.0)
    gates = raised / jnp.sum(raised, 0, keepdims=True)
    before = lax.broadcasted_iota(jnp.int32, (rows, rows), 0) < lanes((rows, rows))
    rank = mm(chosen.astype(BF), before.astype(F32).astype(BF))
    rank = jnp.where(chosen > 0, rank, -1.0)[:8]
    rank_ref[0] = rank
    hot = one_hot(rank, local, capacity)
    low = hot.astype(BF)
    xs_ref[...] = mm(low, h2).astype(BF).reshape(xs_ref.shape)
    gs_ref[...] = mm(low, g_ref[0]).astype(BF).reshape(gs_ref.shape)
    spread = jnp.concatenate(
        [jnp.broadcast_to(gates[e : e + 1], (capacity, rows)) for e in range(local)], 0
    )
    slot_gate = jnp.sum(hot * spread, -1, keepdims=True)
    slot_gate_ref[...] = jnp.broadcast_to(slot_gate, (local * capacity, PAIR)).reshape(
        slot_gate_ref.shape
    )

    @pl.when(unit == own_ref[0])
    def _():
        x1_ref[...] = x1
        h2_ref[...] = h2
        gates_ref[...] = gates


def route(own, o_all, x_all, g_all, w_out, gain, router_t, routes_t, local, capacity):
    units, rows, width = x_all.shape
    groups = o_all.shape[0]
    part = rows // MICRO
    experts = router_t.shape[0]
    slots = pl.BlockSpec((1, local, capacity, width), lambda u, s: (u, 0, 0, 0))
    block = pl.BlockSpec((1, rows, width), lambda u, s: (u, 0, 0))

    def fixed(*shape):
        return pl.BlockSpec(shape, lambda u, s: (0,) * len(shape))

    return pl.pallas_call(
        functools.partial(route_kernel, local, capacity),
        grid_spec=pltpu.PrefetchScalarGridSpec(
            num_scalar_prefetch=1,
            grid=(units,),
            in_specs=[
                pl.BlockSpec((groups, MICRO, part, PAIR), lambda u, s: (0, 0, u, 0)),
                block,
                block,
                fixed(groups * PAIR, width),
                fixed(1, width),
                fixed(experts, width),
                pl.BlockSpec((1, routes_t.shape[1], rows), lambda u, s: (u, 0, 0)),
            ],
            out_specs=[
                slots,
                slots,
                pl.BlockSpec((1, local, capacity, PAIR), lambda u, s: (u, 0, 0, 0)),
                pl.BlockSpec((1, 8, rows), lambda u, s: (u, 0, 0)),
                fixed(rows, width),
                fixed(rows, width),
                fixed(experts, rows),
            ],
        ),
        out_shape=[
            jax.ShapeDtypeStruct((units, local, capacity, width), BF),
            jax.ShapeDtypeStruct((units, local, capacity, width), BF),
            jax.ShapeDtypeStruct((units, local, capacity, PAIR), F32),
            jax.ShapeDtypeStruct((units, 8, rows), F32),
            jax.ShapeDtypeStruct((rows, width), F32),
            jax.ShapeDtypeStruct((rows, width), BF),
            jax.ShapeDtypeStruct((experts, rows), F32),
        ],
        compiler_params=params(),
        cost_estimate=cost(
            2 * units * rows * width * (width + 2 * local * capacity), 14 * units * rows * width
        ),
        name="route",
    )(own, o_all, x_all, g_all, w_out, gain, router_t, routes_t)


def expert_kernel(
    local, experts,
    own_ref, xs_ref, gs_ref, gate_ref, w_ref,
    ys_ref, dx_ref, dg_ref, dw_ref,
):
    expert = pl.program_id(0)
    units, _, capacity, width = xs_ref.shape
    total = units * capacity
    shards, _, _, block, hidden = w_ref.shape
    half = block // 2
    depth = shards * block
    xs = xs_ref[...].reshape(total, width)
    gs = gs_ref[...].reshape(total, width)
    gate = gate_ref[...].reshape(total, PAIR)[:, :1]
    w_gate = w_ref[:, 0, 0].reshape(depth, hidden)
    w_up = w_ref[:, 0, 1].reshape(depth, hidden)
    w_down = jnp.concatenate(
        [w_ref[:, 0, 2, :half].reshape(hidden, hidden), w_ref[:, 0, 2, half:].reshape(hidden, hidden)], 1
    )
    a = mm(xs, w_gate)
    b = mm(xs, w_up)
    sigmoid = jax.nn.sigmoid(a)
    silu = a * sigmoid
    hid = (silu * b).astype(BF)
    y = mm(hid, w_down).astype(BF).astype(F32)
    ys_ref[...] = (gate * y).astype(BF).reshape(ys_ref.shape)
    back = mm(gs, w_down, NT)
    hid_full = hid.astype(F32)
    d_gate = jnp.sum(back * hid_full, -1, keepdims=True)
    d_hid = gate * back
    da = (d_hid * b * sigmoid * (1.0 + a * (1.0 - sigmoid))).astype(BF)
    db = (d_hid * silu).astype(BF)
    dx = mm(da, w_gate, NT) + mm(db, w_up, NT)
    dx_ref[...] = dx.astype(BF).reshape(dx_ref.shape)
    high = d_gate.astype(BF).astype(F32)
    rest = d_gate - high
    shape = (units, capacity, PAIR)
    source = lax.broadcasted_iota(jnp.int32, shape, 0)
    place = (local * (own_ref[0] - source) + expert + experts) % experts
    spot = lanes(shape)
    high = jnp.broadcast_to(high, (total, PAIR)).reshape(shape)
    rest = jnp.broadcast_to(rest, (total, PAIR)).reshape(shape)
    spread = jnp.where(spot == place, high, jnp.where(spot == place + experts, rest, 0.0))
    dg_ref[...] = spread.astype(BF).reshape(dg_ref.shape)
    d_gate_w = mm(xs, da, TN).astype(BF)
    dw_ref[:, 0, 0] = d_gate_w.reshape(shards, block, hidden)
    d_up_w = mm(xs, db, TN).astype(BF)
    dw_ref[:, 0, 1] = d_up_w.reshape(shards, block, hidden)
    scaled = (hid_full * gate).astype(BF)
    d_down_w = mm(scaled, gs, TN).astype(BF)
    dw_ref[:, 0, 2, :half] = d_down_w[:, :hidden].reshape(shards, half, hidden)
    dw_ref[:, 0, 2, half:] = d_down_w[:, hidden:].reshape(shards, half, hidden)


def run_experts(own, xs, gs, gate, weights, experts):
    units, local, capacity, width = xs.shape
    shards, _, kinds, block, hidden = weights.shape
    rows = pl.BlockSpec((units, 1, capacity, width), lambda e, s: (0, e, 0, 0))
    narrow = pl.BlockSpec((units, 1, capacity, PAIR), lambda e, s: (0, e, 0, 0))
    wide = pl.BlockSpec((shards, 1, kinds, block, hidden), lambda e, s: (0, e, 0, 0, 0))
    return pl.pallas_call(
        functools.partial(expert_kernel, local, experts),
        grid_spec=pltpu.PrefetchScalarGridSpec(
            num_scalar_prefetch=1,
            grid=(local,),
            in_specs=[rows, rows, narrow, wide],
            out_specs=[rows, rows, narrow, wide],
        ),
        out_shape=[
            jax.ShapeDtypeStruct(xs.shape, BF),
            jax.ShapeDtypeStruct(xs.shape, BF),
            jax.ShapeDtypeStruct((units, local, capacity, PAIR), BF),
            jax.ShapeDtypeStruct(weights.shape, BF),
        ],
        compiler_params=params(),
        cost_estimate=cost(
            18 * units * local * capacity * width * hidden, 4 * weights.size + 8 * xs.size
        ),
        name="run_experts",
    )(own, xs, gs, gate, weights)


def combine_kernel(local, capacity, rank_ref, ys_ref, dx_ref, dg_ref, mix_ref, grad_ref):
    slots = local * capacity
    width = ys_ref.shape[-1]
    hot = one_hot(rank_ref[0], local, capacity).astype(BF)
    mix_ref[0] = mm(hot, ys_ref[0].reshape(slots, width), TN).astype(BF)
    grad_ref[0, :, :width] = mm(hot, dx_ref[0].reshape(slots, width), TN).astype(BF)
    grad_ref[0, :, width:] = mm(hot, dg_ref[0].reshape(slots, PAIR), TN).astype(BF)


def combine(rank, ys, dx, dg):
    units, local, capacity, width = ys.shape
    rows = rank.shape[-1]
    slots = pl.BlockSpec((1, local, capacity, width), lambda u: (u, 0, 0, 0))
    return pl.pallas_call(
        functools.partial(combine_kernel, local, capacity),
        grid=(units,),
        in_specs=[
            pl.BlockSpec((1, 8, rows), lambda u: (u, 0, 0)),
            slots,
            slots,
            pl.BlockSpec((1, local, capacity, PAIR), lambda u: (u, 0, 0, 0)),
        ],
        out_specs=[
            pl.BlockSpec((1, rows, width), lambda u: (u, 0, 0)),
            pl.BlockSpec((1, rows, width + PAIR), lambda u: (u, 0, 0)),
        ],
        out_shape=[
            jax.ShapeDtypeStruct((units, rows, width), BF),
            jax.ShapeDtypeStruct((units, rows, width + PAIR), BF),
        ],
        compiler_params=params(),
        cost_estimate=cost(4 * units * rows * local * capacity * width, 16 * units * rows * width),
        name="combine",
    )(rank, ys, dx, dg)


def own_kernel(
    own_ref, grad_ref, mix_ref, x1_ref, h2_ref, gates_ref, g_ref, router_ref, gain_ref, wo_ref, o_ref,
    mixed_ref, dx1_ref, do_ref, dwo_ref, dr_ref, dgain_ref,
):
    rows, width = x1_ref.shape
    experts = router_ref.shape[0]
    groups = o_ref.shape[0]
    x1 = x1_ref[...]
    mixed_ref[...] = (x1 + mix_ref[...].astype(F32)).astype(BF)
    flat = grad_ref[:, width:].astype(F32).T
    d_gate = flat[:experts] + flat[experts : 2 * experts]
    gates = gates_ref[...]
    d_logit = gates * (d_gate - jnp.sum(gates * d_gate, 0, keepdims=True))
    router = router_ref[...].astype(F32)
    dh2 = grad_ref[:, :width].astype(F32) + mm(d_logit, router, TN, HIGHEST)
    dr_ref[...] = mm(d_logit, h2_ref[...].astype(F32), NN, HIGHEST)
    scale = lax.rsqrt(jnp.mean(x1 * x1, -1, keepdims=True) + EPSILON)
    normed = x1 * scale
    dgain_ref[...] = jnp.sum(dh2 * normed, 0, keepdims=True)
    dn = dh2 * gain_ref[...]
    dx1 = g_ref[...].astype(F32) + scale * (dn - normed * jnp.mean(dn * normed, -1, keepdims=True))
    dx1_ref[...] = dx1
    dz = dx1.astype(BF)
    grad_o = mm(dz, wo_ref[...], NT).astype(BF)
    heads = jnp.concatenate([o_ref[i].reshape(rows, PAIR) for i in range(groups)], 1)
    dwo = mm(heads, dz, TN).astype(BF)
    for i in range(groups):
        do_ref[i] = grad_o[:, i * PAIR : (i + 1) * PAIR]
        dwo_ref[i] = dwo[:, i * PAIR : (i + 1) * PAIR]


def own_tokens(own, grad, mix, x1, h2, gates, g, router_t, gain, w_out, o_all):
    rows, width = x1.shape
    groups = o_all.shape[0]
    part = rows // MICRO
    experts = router_t.shape[0]

    def fixed(*shape):
        return pl.BlockSpec(shape, lambda i, s: (0,) * len(shape))

    return pl.pallas_call(
        own_kernel,
        grid_spec=pltpu.PrefetchScalarGridSpec(
            num_scalar_prefetch=1,
            grid=(1,),
            in_specs=[
                fixed(*grad.shape),
                fixed(rows, width),
                fixed(rows, width),
                fixed(rows, width),
                fixed(experts, rows),
                fixed(rows, width),
                fixed(experts, width),
                fixed(1, width),
                fixed(groups * PAIR, width),
                pl.BlockSpec((groups, MICRO, part, PAIR), lambda i, s: (0, 0, s[0], 0)),
            ],
            out_specs=[
                fixed(rows, width),
                fixed(rows, width),
                fixed(groups, rows, PAIR),
                fixed(groups, groups * PAIR, PAIR),
                fixed(experts, width),
                fixed(1, width),
            ],
        ),
        out_shape=[
            jax.ShapeDtypeStruct((rows, width), BF),
            jax.ShapeDtypeStruct((rows, width), F32),
            jax.ShapeDtypeStruct((groups, rows, PAIR), BF),
            jax.ShapeDtypeStruct((groups, groups * PAIR, PAIR), BF),
            jax.ShapeDtypeStruct((experts, width), F32),
            jax.ShapeDtypeStruct((1, width), F32),
        ],
        compiler_params=params(),
        cost_estimate=cost(4 * rows * width * width, 20 * rows * width),
        name="own_tokens",
    )(own, grad, mix, x1, h2, gates, g, router_t, gain, w_out, o_all)


def project_back_kernel(x_ref, h_ref, dq_ref, dkv_ref, w_ref, dw_ref, dh_ref, dgain_ref):
    unit = pl.program_id(0)
    rows = x_ref.shape[1]

    @pl.when(unit == 0)
    def _():
        dw_ref[...] = jnp.zeros_like(dw_ref)
        dgain_ref[...] = jnp.zeros_like(dgain_ref)

    grads = jnp.concatenate(
        [dq_ref[...].reshape(rows, PAIR), dkv_ref[...].reshape(rows, PAIR)], 1
    )
    dw_ref[...] += mm(grads, h_ref[0], TN)
    dh = mm(grads, w_ref[...], NT)
    dh_ref[0] = dh.astype(BF)
    x = x_ref[0].astype(F32)
    scale = lax.rsqrt(jnp.mean(x * x, -1, keepdims=True) + EPSILON)
    dgain_ref[...] += jnp.sum(dh * (x * scale), 0, keepdims=True)


def project_back(x_all, h_all, dq, dkv, weight):
    units, rows, width = x_all.shape
    part = rows // MICRO
    block = pl.BlockSpec((1, rows, width), lambda u: (u, 0, 0))
    place = pl.BlockSpec((MICRO, part, PAIR), lambda u: (0, u, 0))
    return pl.pallas_call(
        project_back_kernel,
        grid=(units,),
        in_specs=[block, block, place, place, pl.BlockSpec((width, 2 * PAIR), lambda u: (0, 0))],
        out_specs=[
            pl.BlockSpec((2 * PAIR, width), lambda u: (0, 0)),
            block,
            pl.BlockSpec((1, width), lambda u: (0, 0)),
        ],
        out_shape=[
            jax.ShapeDtypeStruct((2 * PAIR, width), F32),
            jax.ShapeDtypeStruct((units, rows, width), BF),
            jax.ShapeDtypeStruct((1, width), F32),
        ],
        compiler_params=params(),
        cost_estimate=cost(8 * units * rows * width * PAIR, 6 * units * rows * width),
        name="project_back",
    )(x_all, h_all, dq.reshape(MICRO, -1, PAIR), dkv.reshape(MICRO, -1, PAIR), weight)


def per_device(
    tokens,
    routes,
    doc_starts,
    attn_gain,
    attn_q,
    attn_k,
    attn_v,
    attn_out,
    ffn_gain,
    router,
    w_gate,
    w_up,
    w_down,
    cotangent,
):
    part = tokens.shape[2]
    width = tokens.shape[3]
    top = routes.shape[3]
    experts = router.shape[1]
    local, shard, hidden = w_gate.shape
    units = lax.axis_size("ctx")
    shards = lax.axis_size("fsdp")
    rank = lax.axis_index("ctx")
    rows = MICRO * part
    length = units * rows
    capacity = MICRO * (5 * part * top // (4 * experts))
    own = rank.astype(jnp.int32).reshape(1)

    def gather_ctx(block):
        return lax.all_gather(block, "ctx", axis=0, tiled=False)

    piece = shard * PAIR // PAIR
    columns = jnp.concatenate(
        [
            lax.dynamic_slice_in_dim(attn_q, rank * PAIR, PAIR, 1),
            lax.dynamic_slice_in_dim(attn_k, rank * HEAD_DIM, HEAD_DIM, 1),
            lax.dynamic_slice_in_dim(attn_v, rank * HEAD_DIM, HEAD_DIM, 1),
            lax.dynamic_slice_in_dim(attn_out, rank * PAIR, PAIR, 1),
        ],
        1,
    )
    small = jnp.concatenate([attn_gain, ffn_gain, router.reshape(-1)])
    wide = columns.shape[1]
    extra = -(-small.shape[0] // (8 * wide)) * 8
    small = jnp.pad(small, (0, extra * wide - small.shape[0])).reshape(extra, wide)
    dense = lax.all_gather(jnp.concatenate([columns, small], 0), "fsdp", axis=0, tiled=False)
    columns = dense[:, :piece].reshape(shards * shard, wide)
    w_qkv = columns[:, : 2 * PAIR]
    w_out_part = columns[:, 2 * PAIR :]
    small = dense[:, piece:].reshape(shards, -1)
    gain_one = small[:, :shard].reshape(1, width).astype(F32)
    gain_two = small[:, shard : 2 * shard].reshape(1, width).astype(F32)
    router_all = small[:, 2 * shard : 2 * shard + shard * experts].reshape(width, experts)
    router_t = jnp.roll(router_all.T, -local * rank, 0)

    expert_pack = jnp.stack(
        [w_gate, w_up, jnp.concatenate([w_down[..., :hidden], w_down[..., hidden:]], 1)], 1
    )
    weights = lax.all_gather(expert_pack, "fsdp", axis=0, tiled=False)

    x_own = tokens[0].reshape(rows, width)
    g_own = cotangent[0].reshape(rows, width)
    x_all = gather_ctx(x_own)
    g_all = gather_ctx(g_own)
    w_out = gather_ctx(w_out_part).transpose(1, 0, 2).reshape(units * PAIR, width)
    index = jnp.concatenate([routes[0].reshape(rows, top).T, doc_starts[0].reshape(1, rows)], 0)
    index = gather_ctx(index)
    routes_t = (index[:, :top] - local * rank) % experts
    starts = index[:, top].reshape(units, MICRO, part).transpose(1, 0, 2).reshape(1, length)

    cosine, sine = angle_tables(length)
    q, kv, h_all = project(x_all, w_qkv, gain_one, cosine, sine)
    q = q.reshape(length, PAIR)
    kv = kv.reshape(length, PAIR)
    o, lse = attend(q, kv, starts)
    o_all = gather_ctx(o).reshape(units, MICRO, length // MICRO, PAIR)
    xs, gs, slot_gate, ranks, x1, h2, gates = route(
        own, o_all, x_all, g_all, w_out, gain_two, router_t, routes_t, local, capacity
    )
    ys, dx, dg, dw = run_experts(own, xs, gs, slot_gate, weights, experts)
    mix, grad = combine(ranks, ys, dx, dg)
    grad = lax.psum_scatter(grad, "ctx", scatter_dimension=0, tiled=True)[0]
    mix = lax.psum_scatter(mix, "ctx", scatter_dimension=0, tiled=True)[0]
    mixed, dx1, grad_o, dwo, d_router, d_gain_two = own_tokens(
        own, grad, mix, x1, h2, gates, g_own, router_t, gain_two, w_out, o_all
    )
    grad_o = lax.all_to_all(grad_o, "ctx", split_axis=0, concat_axis=0, tiled=True)
    grad_o = grad_o.reshape(units, MICRO, part, PAIR)
    dwo = lax.psum_scatter(dwo, "ctx", scatter_dimension=0, tiled=True)[0]
    dq, dkv = attend_back(q, kv, starts, lse, o, grad_o, cosine, sine)
    dw_qkv, dh, d_gain_one = project_back(x_all, h_all, dq, dkv, w_qkv)
    dh = lax.psum_scatter(dh, "ctx", scatter_dimension=0, tiled=True)[0].astype(F32)

    x = x_own.astype(F32)
    scale = lax.rsqrt(jnp.mean(x * x, -1, keepdims=True) + EPSILON)
    normed = x * scale
    dn = dh * gain_one
    d_tokens = dx1 + scale * (dn - normed * jnp.mean(dn * normed, -1, keepdims=True))

    pack = jnp.concatenate(
        [
            dw_qkv.T.astype(BF),
            dwo.astype(BF),
            jnp.roll(d_router, local * rank, 0).T.astype(BF),
            d_gain_one.T.astype(BF),
            d_gain_two.T.astype(BF),
        ],
        1,
    )
    used = pack.shape[1]
    pack = jnp.pad(pack, ((0, 0), (0, -used % PAIR))).reshape(shards, shard, -1)
    pack = lax.all_to_all(pack, "fsdp", split_axis=0, concat_axis=0, tiled=True)
    pack = jnp.sum(pack.astype(F32), 0).astype(BF)
    pack = gather_ctx(pack).astype(F32)

    def wide_columns(first, count):
        return pack[:, :, first : first + count].transpose(1, 0, 2).reshape(shard, units * count)

    def summed(first, count):
        return jnp.sum(pack[:, :, first : first + count], 0)

    dw = lax.psum_scatter(dw, "fsdp", scatter_dimension=0, tiled=True)[0].astype(F32)
    d_down = dw[:, 2]
    d_down = jnp.concatenate([d_down[:, : shard // 2], d_down[:, shard // 2 :]], -1)
    first_small = 3 * PAIR
    return (
        mixed.reshape(1, MICRO, part, width),
        d_tokens.reshape(1, MICRO, part, width),
        summed(first_small + experts, 1).reshape(shard),
        wide_columns(0, PAIR),
        wide_columns(PAIR, HEAD_DIM),
        wide_columns(PAIR + HEAD_DIM, HEAD_DIM),
        wide_columns(2 * PAIR, PAIR),
        summed(first_small + experts + 1, 1).reshape(shard),
        summed(first_small, experts),
        dw[:, 0],
        dw[:, 1],
        d_down,
    )


def solution(mesh):
    return jax.shard_map(
        per_device,
        mesh=mesh,
        in_specs=(
            P("fsdp", None, "ctx", None),
            P("fsdp", None, "ctx", None),
            P("fsdp", None, "ctx"),
            P("fsdp"),
            P("fsdp", None),
            P("fsdp", None),
            P("fsdp", None),
            P("fsdp", None),
            P("fsdp"),
            P("fsdp", None),
            P("ctx", "fsdp", None),
            P("ctx", "fsdp", None),
            P("ctx", "fsdp", None),
            P("fsdp", None, "ctx", None),
        ),
        out_specs=(
            P("fsdp", None, "ctx", None),
            P("fsdp", None, "ctx", None),
            P("fsdp"),
            P("fsdp", None),
            P("fsdp", None),
            P("fsdp", None),
            P("fsdp", None),
            P("fsdp"),
            P("fsdp", None),
            P("ctx", "fsdp", None),
            P("ctx", "fsdp", None),
            P("ctx", "fsdp", None),
        ),
        check_vma=False,
    )
```

time: 1660 us -> 576 us (0.35)
  waiting for transfers between devices: 935 us -> 302 us
  matrix products: 200 us -> 0 us
  blocking collectives: 188 us -> 52.7 us
  Pallas kernels: 0 us -> 135 us
  other arithmetic: 141 us -> 23.3 us
  local copies, waits for them, and re-layouts: 148 us -> 35.9 us
    reduce_scatter x7 -> x4, waiting for transfers between devices: 519 us -> 77.8 us  [the longest x1 40.6 us: per_device(): grad = lax.psum_scatter(grad, 'ctx', scatter_dimension=0, tiled=True)[0]]
    dot_general x72 -> x0, matrix products: 200 us -> none  [the longest x2 18.7 us: per_device(): jnp.einsum('qgcd,jgd->gcqj', grad_grouped, value_part, preferred_element_...]
    pallas_call x0 -> x8, Pallas kernels: none -> 135 us  [the longest x1 34.1 us: run_experts(): pl.pallas_call(functools.partial(expert_kernel, local, experts), grid_spe...]
    all_gather x9 -> x5, waiting for transfers between devices: 207 us -> 116 us  [the longest x1 74.4 us: per_device(): weights = lax.all_gather(expert_pack, 'fsdp', axis=0, tiled=False)]
    unnamed x2 -> x0, blocking collectives: 79.1 us -> none
    all_to_all x2 -> x0, blocking collectives: 72.6 us -> none  [to_owners(): lax.all_to_all(slot_rows, 'ctx', split_axis=0, concat_axis=0, tiled=True)]
    all_to_all x6 -> x2, waiting for transfers between devices: 74.3 us -> 21.1 us  [the longest x1 16.4 us: per_device(): pack = lax.all_to_all(pack, 'fsdp', split_axis=0, concat_axis=0, tiled=True)]
    unnamed x21 -> x11, waiting for transfers between devices: 134 us -> 87.2 us
  transfers between devices with their start and end apart: 25 -> 12, of which waited for: 20 -> 8; matrix products, arithmetic and copies ran while one was open for 18% -> 7% of each run, Pallas kernels for 0% -> 14%
where the time goes in v1:
time: 576 us; the launch traced here: 574 us
  waiting for transfers between devices  302 us (52%)
  Pallas kernels  135 us (23%)
  blocking collectives  52.7 us (9%)
  local copies, waits for them, and re-layouts  35.9 us (6%)
  other arithmetic  23.3 us (4%)
  between operations  14.6 us (3%)
  starting transfers between devices  11.1 us (2%)
    unnamed x11, waiting for transfers between devices  87.2 us
    all_gather x1, waiting for transfers between devices, per_device(): weights = lax.all_gather(expert_pack, 'fsdp', axis=0, tiled=False)  74.4 us
    all_gather x4, waiting for transfers between devices, gather_ctx(): return lax.all_gather(block, 'ctx', axis=0, tiled=False)  41.3 us
    reduce_scatter x1, waiting for transfers between devices, per_device(): grad = lax.psum_scatter(grad, 'ctx', scatter_dimension=0, tiled=True)[0]  40.6 us
    reduce_scatter x1, waiting for transfers between devices, per_device(): mix = lax.psum_scatter(mix, 'ctx', scatter_dimension=0, tiled=True)[0]  37.2 us
    pallas_call x1, Pallas kernels, run_experts(): pl.pallas_call(functools.partial(expert_kernel, local, experts), grid_spe...  34.1 us
    all_gather x2, blocking collectives, gather_ctx(): return lax.all_gather(block, 'ctx', axis=0, tiled=False)  27.8 us
    pallas_call x1, Pallas kernels, attend_back(): pl.pallas_call(attend_back_kernel, grid=(tiles,), in_specs=[pl.BlockSpec(...  25.5 us
  transfers between devices with their start and end apart: 12, of which 8 were waited for; matrix products, arithmetic and copies ran while one was open for 7% of the time, Pallas kernels for 14%

profile of v1, /device:TPU:0, one launch (start us, length us, event | category | flops | bytes accessed | tf_op | source)
XLA Modules:
  0.0 574.2 jit_solution(8956687475870862048)
XLA Ops:
  12.0 24.9 %all-gather = bf16[1152,384]{1,0:T(8,128)(2,1)S(1)} all-gather(bf16[72,384]{1,0:T(8,128)(2,1)S(1)} %pad_maximum_fusion.6), channel_id=2, replica_groups=mesh['ctx'=8,'fsdp'=16] {'fsdp'}, dimensions={0}, use_global_device_ids=true | all-gather | bytes 940032 | tf_op jit(solution)/shard_map/all_gather | solution.py:692
  40.2 14.1 %all-gather.6 = s32[8,9,256]{2,1,0:T(8,128)S(1)} all-gather(s32[1,9,256]{2,1,0:T(8,128)S(1)} %add_bitcast_fusion), channel_id=3, replica_groups=mesh['ctx'=8,'fsdp'=16] {'ctx'}, dimensions={0}, use_global_device_ids=true | all-gather | bytes 82944 | tf_op jit(solution)/shard_map/all_gather | solution.py:676
  54.9 3.7 fusion.5
  61.6 9.2 %project.1 = (bf16[2,1024,128]{2,1,0:T(8,128)(2,1)}, bf16[2,1024,128]{2,1,0:T(8,128)(2,1)}, bf16[8,256,1024]{2,1,0:T(8,128)(2,1)}) custom-call(bf16[8,256,1024]{2,1,0:T(8,128)(2,1)} %all-gather.13.cloned.1.call-done.x_ref, bf16[1024,256]{1,0:T(8,128)(2,1)} %slice.93.w_ref, f32[1,1024]{1,0:T(1,128)} %reshape.292.gain_ref, ...), custom_call_target="tpu_custom_call" | custom-call | flops 1073741824 | bytes 8388608 | tf_op jit(solution)/shard_map/project/pallas_call | solution.py:87
  70.9 20.7 %attend.1 = (bf16[2048,128]{1,0:T(8,128)(2,1)}, f32[8,1,512]{2,1,0:T(1,128)}) custom-call(bf16[2048,128]{1,0:T(8,128)(2,1)} %bitcast.126, bf16[8,256,128]{2,1,0:T(8,128)(2,1)} %bitcast.128, s32[8,1,256]{2,1,0:T(1,128)} %bitcast.122), custom_call_target="tpu_custom_call" | custom-call | flops 4294967296 | bytes 2097152 | tf_op jit(solution)/shard_map/attend/pallas_call | solution.py:180
  99.0 7.6 %all-gather.15.cloned.1.call-done.g_ref = bf16[8,256,1024]{2,1,0:T(8,128)(2,1)} async-done(((bf16[1,256,1024]{2,1,0:T(8,128)(2,1)}), bf16[8,256,1024]{2,1,0:T(8,128)(2,1)}) %all-gather.15.cloned.1.call-update) | async-done | bytes 4194320 | tf_op jit(solution)/shard_map/all_gather | solution.py:676
  106.6 33.7 %all-gather.17.cloned.1.call-done = bf16[16384,128]{1,0:T(8,128)(2,1)} async-done(((bf16[2048,128]{1,0:T(8,128)(2,1)}), bf16[16384,128]{1,0:T(8,128)(2,1)}) %all-gather.17.cloned.1.call-update) | async-done | bytes 4194320 | tf_op jit(solution)/shard_map/all_gather | solution.py:676
  140.3 17.3 %route.1 = (bf16[8,4,80,1024]{3,2,1,0:T(8,128)(2,1)}, bf16[8,4,80,1024]{3,2,1,0:T(8,128)(2,1)}, f32[8,4,80,128]{3,2,1,0:T(8,128)}, f32[8,8,256]{2,1,0:T(8,128)},...) custom-call(s32[1]{0:T(128)} %bitcast.own_ref, bf16[8,2,1024,128]{3,2,1,0:T(8,128)(2,1)} %bitcast.96, ...), custom_call_target="tpu_custom_call" | custom-call | flops 6979321856 | bytes 29360128 | tf_op jit(solution)/shard_map/route/pallas_call | solution.py:362
  157.6 74.4 %all-gather.21.cloned.1.call-done = bf16[64,3,64,512]{3,2,0,1:T(8,128)(2,1)} async-done(((bf16[4,3,64,512]{3,2,0,1:T(8,128)(2,1)}), bf16[64,3,64,512]{3,2,0,1:T(8,128)(2,1)}) %all-gather.21.cloned.1.call-update) | async-done | bytes 12582928 | tf_op jit(solution)/shard_map/all_gather | solution.py:705
  232.0 10.8 %copy.64 = bf16[64,3,64,512]{3,2,1,0:T(8,128)(2,1)} copy(bf16[64,3,64,512]{3,2,0,1:T(8,128)(2,1)} %all-gather.21.cloned.1.call-done) | data formatting | bytes 25165824 | tf_op jit(solution)/shard_map/all_gather | solution.py:705
  242.8 34.1 %run_experts.1 = (bf16[8,4,80,1024]{3,2,1,0:T(8,128)(2,1)}, bf16[8,4,80,1024]{3,2,1,0:T(8,128)(2,1)}, bf16[8,4,80,128]{3,2,1,0:T(8,128)(2,1)}, bf16[16,4,3,64,512]{4,3,2,1,0:T(8,128)(2,1)}) custom-call(s32[1]{0:T(128)} %bitcast.own_ref, bf16[8,4,80,1024]{3,2,1,0:T(8,128)(2,1)} %get-tuple-element.45.xs_ref, ...), custom_call_target="tpu_custom_call" | custom-call | flops 24159191040 | bytes 46137344 | tf_op jit(solution)/shard_map/run_experts/pallas_call | solution.py:463
  277.0 11.3 %combine.1 = (bf16[8,256,1024]{2,1,0:T(8,128)(2,1)}, bf16[8,256,1152]{2,1,0:T(8,128)(2,1)}) custom-call(f32[8,8,256]{2,1,0:T(8,128)} %get-tuple-element.44.rank_ref, bf16[8,4,80,1024]{3,2,1,0:T(8,128)(2,1)} %get-tuple-element.48.ys_ref, bf16[8,4,80,1024]{3,2,1,0:T(8,128)(2,1)} %get-tuple-element.49.dx_ref, bf16[8,4,80,128]{3,2,1,0:T(8,128)(2,1)} %get-tuple-element.50.dg_ref), custom_call_target="tpu_custom_call" | custom-call | flops 2684354560 | bytes 33554432 | tf_op jit(solution)/shard_map/combine/pallas_call | solution.py:498
  289.1 37.2 %reduce-scatter.10.cloned.1.call-done = bf16[1,256,1024]{2,1,0:T(8,128)(2,1)} async-done(((bf16[8,256,1024]{2,1,0:T(8,128)(2,1)}), bf16[1,256,1024]{2,1,0:T(8,128)(2,1)}) %reduce-scatter.10.cloned.1.call-update) | async-done | bytes 524304 | tf_op jit(solution)/shard_map/reduce_scatter | solution.py:729
  326.3 40.6 %reduce-scatter.8.cloned.1.call-done = bf16[1,256,1152]{2,1,0:T(8,128)(2,1)} async-done(((bf16[8,256,1152]{2,1,0:T(8,128)(2,1)}), bf16[1,256,1152]{2,1,0:T(8,128)(2,1)}) %reduce-scatter.8.cloned.1.call-update) | async-done | bytes 589840 | tf_op jit(solution)/shard_map/reduce_scatter | solution.py:728
  366.9 7.0 %own_tokens.1 = (bf16[256,1024]{1,0:T(8,128)(2,1)}, f32[256,1024]{1,0:T(8,128)}, bf16[8,256,128]{2,1,0:T(8,128)(2,1)}, bf16[8,1024,128]{2,1,0:T(8,128)(2,1)}, f32[32,1024]{1,0:T(8,128)}, /*index=5*/f32[1,1024]{1,0:T(1,128)}) custom-call(s32[1]{0:T(128)} %bitcast.own_ref, bf16[256,1152]{1,0:T(8,128)(2,1)} %bitcast.106, bf16[256,1024]{1,0:T(8,128)(2,1)} %bitcast.107, ...), custom_call_target="tpu_custom_call" | custom-call | flops 1073741824 | bytes 5242880 | tf_op jit(solution)/shard_map/own_tokens/pallas_call | solution.py:561
  373.9 3.9 copy.66
  381.6 3.7 fusion.6
  388.4 4.6 all-to-all-done
  393.8 25.5 %attend_back.1 = (bf16[2048,128]{1,0:T(8,128)(2,1)}, bf16[2048,128]{1,0:T(8,128)(2,1)}) custom-call(bf16[2048,128]{1,0:T(8,128)(2,1)} %bitcast.127, bf16[8,256,128]{2,1,0:T(8,128)(2,1)} %bitcast.129, s32[8,1,256]{2,1,0:T(1,128)} %bitcast.123, f32[8,1,512]{2,1,0:T(1,128)} %get-tuple-element.59.lse_ref, bf16[2048,128]{1,0:T(8,128)(2,1)} %get-tuple-element.43.o_ref, ...), custom_call_target="tpu_custom_call" | custom-call | flops 10737418240 | bytes 4194304 | tf_op jit(solution)/shard_map/attend_back/pallas_call | solution.py:273
  419.3 9.5 %project_back.1 = (f32[256,1024]{1,0:T(8,128)}, bf16[8,256,1024]{2,1,0:T(8,128)(2,1)}, f32[1,1024]{1,0:T(1,128)}) custom-call(bf16[8,256,1024]{2,1,0:T(8,128)(2,1)} %all-gather.13.cloned.1.call-done.x_ref, bf16[8,256,1024]{2,1,0:T(8,128)(2,1)} %get-tuple-element.58.h_ref, bf16[2,1024,128]{2,1,0:T(8,128)(2,1)} %bitcast.108, bf16[2,1024,128]{2,1,0:T(8,128)(2,1)} %bitcast.109, ...), custom_call_target="tpu_custom_call" | custom-call | flops 2147483648 | bytes 12582912 | tf_op jit(solution)/shard_map/project_back/pallas_call | solution.py:626
  433.1 6.8 %all-to-all-start.1 = ((bf16[16,64,512]{2,1,0:T(8,128)(2,1)}), bf16[16,64,512]{2,1,0:T(8,128)(2,1)S(1)}, u32[]{:S(2)}, u32[]{:S(2)}) async-start(bf16[16,64,512]{2,1,0:T(8,128)(2,1)} %bitcast.39), calls=%async_computation.5 | async-start | bytes 2097152 | tf_op jit(solution)/shard_map/all_to_all | solution.py:758
  440.2 16.4 %all-to-all-done.1 = bf16[16,64,512]{2,1,0:T(8,128)(2,1)S(1)} async-done(((bf16[16,64,512]{2,1,0:T(8,128)(2,1)}), bf16[16,64,512]{2,1,0:T(8,128)(2,1)S(1)}, u32[]{:S(2)}, u32[]{:S(2)}) %all-to-all-start.1) | async-done | bytes 1048608 | tf_op jit(solution)/shard_map/all_to_all | solution.py:758
  456.8 13.7 %all-gather.5 = bf16[512,512]{1,0:T(8,128)(2,1)S(1)} all-gather(bf16[64,512]{1,0:T(8,128)(2,1)S(1)} %reduce_sum.59), channel_id=7, replica_groups=mesh['ctx'=8,'fsdp'=16] {'ctx'}, dimensions={0}, use_global_device_ids=true | all-gather | bytes 589824 | tf_op jit(solution)/shard_map/all_gather | solution.py:676
  479.4 84.6 %reduce-scatter.16.cloned.1.call-done = bf16[1,4,3,64,512]{4,3,2,1,0:T(8,128)(2,1)} async-done(((bf16[16,4,3,64,512]{4,3,2,1,0:T(8,128)(2,1)}), bf16[1,4,3,64,512]{4,3,2,1,0:T(8,128)(2,1)}) %reduce-scatter.16.cloned.1.call-update) | async-done | bytes 786448
  (112 shorter events, 44.1 us)
Async XLA Ops:
  7.2 33.0 %copy-start.8 = (s32[1,2,128,8]{2,3,1,0:T(8,128)S(1)}, s32[1,2,128,8]{2,3,1,0:T(8,128)}, u32[]{:S(2)}) copy-start(s32[1,2,128,8]{2,3,1,0:T(8,128)} %param.15) | copy-start | bytes 24580
  7.2 33.0 %copy-start.11 = (s32[1,2,128]{2,1,0:T(2,128)S(1)}, s32[1,2,128]{2,1,0:T(2,128)}, u32[]{:S(2)}) copy-start(s32[1,2,128]{2,1,0:T(2,128)} %param.16) | copy-start | bytes 3076
  7.2 54.4 %all-gather.13.cloned.1.call-start = ((), (), s32[]{:S(2)}) async-start(), calls=%async_computation.7 | async-start | bytes 4718592 | tf_op jit(solution)/shard_map/all_gather | solution.py:676
  7.9 87.5 %all-gather.19.cloned.1.call-start = ((), (), s32[]{:S(2)}) async-start(), calls=%async_computation.14 | async-start | bytes 2359296 | tf_op jit(solution)/shard_map/all_gather | solution.py:676
  37.8 68.8 %all-gather.15.cloned.1.call-start = ((), (), s32[]{:S(2)}) async-start(), calls=%async_computation.8 | async-start | bytes 4718592 | tf_op jit(solution)/shard_map/all_gather | solution.py:676
  38.5 101.8 %all-gather.17.cloned.1.call-start = ((), (), s32[]{:S(2)}) async-start(), calls=%async_computation.13 | async-start | bytes 4718592 | tf_op jit(solution)/shard_map/all_gather | solution.py:676
  70.9 20.8 %copy-start.4 = (bf16[4,32,1024]{2,1,0:T(8,128)(2,1)S(1)}, bf16[4,32,1024]{2,1,0:T(8,128)(2,1)}, u32[]{:S(2)}) copy-start(bf16[4,32,1024]{2,1,0:T(8,128)(2,1)} %param.26) | copy-start | bytes 786436
  70.9 20.9 %copy-start.5 = (bf16[4,64,512]{2,1,0:T(8,128)(2,1)S(1)}, bf16[4,64,512]{2,1,0:T(8,128)(2,1)}, u32[]{:S(2)}) copy-start(bf16[4,64,512]{2,1,0:T(8,128)(2,1)} %param.25) | copy-start | bytes 786436
  70.9 20.9 %copy-start.6 = (bf16[4,64,512]{2,1,0:T(8,128)(2,1)S(1)}, bf16[4,64,512]{2,1,0:T(8,128)(2,1)}, u32[]{:S(2)}) copy-start(bf16[4,64,512]{2,1,0:T(8,128)(2,1)} %param.24) | copy-start | bytes 786436
  91.7 140.4 %all-gather.21.cloned.1.call-start = ((), (), s32[]{:S(2)}) async-start(), calls=%async_computation.15 | async-start | bytes 13369344 | tf_op jit(solution)/shard_map/all_gather | solution.py:705
  92.8 233.5 %reduce-scatter.10.cloned.1.call-start = ((), (), s32[]{:S(2)}) async-start(), calls=%async_computation.10 | async-start | bytes 4718592 | tf_op jit(solution)/shard_map/reduce_scatter | solution.py:729
  288.3 78.6 %reduce-scatter.8.cloned.1.call-start = ((), (), s32[]{:S(2)}) async-start(), calls=%async_computation.9 | async-start | bytes 5308416 | tf_op jit(solution)/shard_map/reduce_scatter | solution.py:728
  289.0 141.2 %reduce-scatter.14.cloned.1.call-start = ((), (), s32[]{:S(2)}) async-start(), calls=%async_computation.12 | async-start | bytes 2359296 | tf_op jit(solution)/shard_map/reduce_scatter | solution.py:735
  377.8 15.2 %all-to-all-start = ((bf16[8,256,128]{2,1,0:T(8,128)(2,1)}), bf16[8,256,128]{2,1,0:T(8,128)(2,1)S(1)}, u32[]{:S(2)}, u32[]{:S(2)}) async-start(bf16[8,256,128]{2,1,0:T(8,128)(2,1)} %get-tuple-element.60), calls=%async_computation.2 | async-start | bytes 1048576 | tf_op jit(solution)/shard_map/all_to_all | solution.py:733
  381.4 94.3 %reduce-scatter.12.cloned.1.call-start = ((), (), s32[]{:S(2)}) async-start(), calls=%async_computation.11 | async-start | bytes 4718592 | tf_op jit(solution)/shard_map/reduce_scatter | solution.py:738
  393.0 0.8 copy-start.3
  428.8 135.2 %reduce-scatter.16.cloned.1.call-start = ((), (), s32[]{:S(2)}) async-start(), calls=%async_computation.16 | async-start | bytes 13369344
  428.8 0.9 copy-start.7
  428.9 0.9 copy-start.9
  428.9 1.0 copy-start.10
  428.9 1.3 copy-start.1
  430.3 9.8 %copy-start = (bf16[1,2,128,1024]{3,2,1,0:T(8,128)(2,1)S(1)}, bf16[1,2,128,1024]{3,2,1,0:T(8,128)(2,1)}, u32[]{:S(2)}) copy-start(bf16[1,2,128,1024]{3,2,1,0:T(8,128)(2,1)} %param.14) | copy-start | bytes 1572868
  433.1 23.5 %all-to-all-start.1 = ((bf16[16,64,512]{2,1,0:T(8,128)(2,1)}), bf16[16,64,512]{2,1,0:T(8,128)(2,1)S(1)}, u32[]{:S(2)}, u32[]{:S(2)}) async-start(bf16[16,64,512]{2,1,0:T(8,128)(2,1)} %bitcast.39), calls=%async_computation.5 | async-start | bytes 2097152 | tf_op jit(solution)/shard_map/all_to_all | solution.py:758
  470.5 6.6 %copy-start.2 = (f32[256,1024]{1,0:T(8,128)S(1)}, f32[256,1024]{1,0:T(8,128)}, u32[]{:S(2)}) copy-start(f32[256,1024]{1,0:T(8,128)} %get-tuple-element.57) | copy-start | bytes 3145732
Sparse Core Ops, SparseCore 0:
  9.7 34.7 all-gather.12
  46.9 25.1 all-gather.18
  73.8 32.7 all-gather.14
  108.2 32.0 all-gather.16
  142.3 89.6 all-gather.20
  288.4 37.8 reduce-scatter.9
  328.7 38.1 reduce-scatter.7
  378.0 34.9 reduce-scatter.13
  428.9 38.7 reduce-scatter.11
  471.0 93.0 reduce-scatter.15
